TPU v7x, 32 devices: a whole 2x2x4 slice. The times are simulated.
32 devices in a mesh: groups: 2 (over x), mp: 8 (over z, y), dp: 2 (over core).
Axes of the slice: x: 2, y: 2, z: 4, core: 2. Of those that a mesh axis runs over, the one named last changes fastest.
Arguments:
- acts: bfloat16 [512, 4096], P(('groups', 'dp')), parts along dimension 0, may hold values from -6 to 6
- out_grads: bfloat16 [512, 14336], P(('groups', 'dp'), 'mp'), parts along dimension 0, may hold values from -6 to 6
- basis_in: bfloat16 [4096, 4096], P(None, 'mp'), may hold values from -0.09375 to 0.09375
- basis_out: bfloat16 [14336, 14336], P('mp', 'dp'), may hold values from -0.046875 to 0.046875
- eigen: float32 [4096, 14336], P(None, ('dp', 'mp')), may hold values from 1 to 16
- lengths: int32 [16], P('groups'), parts along dimension 0, may hold values from 1 to 64, 256 in all
Outputs:
- preconditioned: bfloat16 [16, 32, 14336], P('groups', None, ('mp', 'dp')), parts along dimension 0
There are 2 independent parts, one for each index of `groups`. A program takes and returns all parts, laid end to end along the dimension named above; an argument that names none is the same for every part. Nothing has to cross between parts.
Inputs may be any that keep to these rules, and one draw needn't show every extreme that they name: The sequences lie end to end in the 256 token rows; the lengths sum to 256 and the longest is exactly 64.
All inputs are finite; a program needn't handle non-finite values.
Results may differ from a plain program's by a relative error of at most 0.006.
Values may be sent and summed in bfloat16 or wider, within the bound.
A program may use at most 256 MiB of HBM per device.

v0:
```python
import jax
import jax.numpy as jnp
from jax import lax
from jax.sharding import PartitionSpec as P

OUT_ROWS = 32


def on_device(acts, out_grads, basis_in, basis_out, eigen, lengths):
    rot_local = jnp.dot(acts, basis_in, preferred_element_type=jnp.float32).astype(jnp.bfloat16)
    rot_in, grads_all = (
        lax.all_gather(rot_local, "dp", axis=0, tiled=True),
        lax.all_gather(out_grads, "dp", axis=0, tiled=True),
    )
    total_rows = rot_in.shape[0]
    panel = basis_out
    rot_out = lax.psum_scatter(
        lax.dot_general(
            panel, grads_all, (((0,), (1,)), ((), ())), preferred_element_type=jnp.float32
        ),
        "mp",
        scatter_dimension=0,
        tiled=True,
    ).astype(jnp.bfloat16)
    seq_ends = jnp.cumsum(lengths)
    seq_starts = seq_ends - lengths
    rows_back = basis_in[:OUT_ROWS]
    span = total_rows // 4
    anchor = jnp.minimum(seq_starts, total_rows - span)
    offsets = anchor[:, None] + jnp.arange(span, dtype=jnp.int32)[None, :]
    inside = ((offsets >= seq_starts[:, None]) & (offsets < seq_ends[:, None])).astype(jnp.bfloat16)

    def out_window(root):
        return lax.dynamic_slice_in_dim(rot_out, root, span, 1)

    out_windows = jax.vmap(out_window)(anchor) * inside[:, None, :]
    feat_piece = lax.all_gather(rot_in, "mp", axis=1, tiled=True)
    back_piece = lax.all_gather(rows_back, "mp", axis=1, tiled=True)

    def feat_window(root):
        return lax.dynamic_slice_in_dim(feat_piece, root, span, 0)

    feat_windows = jax.vmap(feat_window)(anchor)
    scaled = (
        jnp.einsum("swk,sjw->skj", feat_windows, out_windows, preferred_element_type=jnp.float32)
        / eigen[None, :, :]
    ).astype(jnp.bfloat16)
    folded = jnp.einsum("ok,skj->soj", back_piece, scaled, preferred_element_type=jnp.float32)
    back_rot = folded.astype(jnp.bfloat16)
    panel = basis_out
    partial_out = jnp.einsum(
        "sok,fk->sof",
        lax.all_gather(back_rot, "mp", axis=2, tiled=True),
        panel,
        preferred_element_type=jnp.float32,
    )
    return lax.psum_scatter(partial_out, "dp", scatter_dimension=2, tiled=True).astype(jnp.bfloat16)


def solution(mesh):
    placed = (
        P(("groups", "dp"), None),
        P(("groups", "dp"), "mp"),
        P(None, "mp"),
        P("mp", "dp"),
        P(None, ("dp", "mp")),
        P("groups"),
    )
    return jax.shard_map(
        on_device,
        mesh=mesh,
        in_specs=placed,
        out_specs=P("groups", None, ("mp", "dp")),
        check_vma=False,
    )
```

profile of v0, /device:TPU:0, one launch (start us, length us, event | category | flops | bytes accessed | tf_op | source)
XLA Modules:
  0.0 345.2 jit_solution(15873830703163142523)
XLA Ops:
  6.5 1.2 copy-done
  7.8 2.9 convolution_convert_fusion
  10.7 2.2 all_gather.15
  13.0 2.5 all_gather.17
  15.4 13.8 %fusion.22 = f32[7168,256]{1,0:T(8,128)} fusion(bf16[1792,7168]{1,0:T(8,128)(2,1)} %param.9, bf16[256,1792]{1,0:T(8,128)(2,1)S(1)} %all_gather.17), kind=kOutput, calls=%fused_computation.25 | convolution fusion | flops 6576668672 | bytes 33947648 | tf_op jit(solution)/shard_map/dot_general | solution.py:18
  29.4 0.6 copy-done.3
  30.2 33.6 %all_gather.18 = bf16[32,4096]{1,0:T(8,128)(2,1)S(1)} all-gather(bf16[32,512]{1,0:T(8,128)(2,1)S(1)} %slice-done), channel_id=1, replica_groups=mesh['groups'=2,'mp'=8,'dp'=2] {'mp'}, dimensions={1}, use_global_device_ids=true | all-gather | bytes 294912 | tf_op jit(solution)/shard_map/all_gather | solution.py:38
  63.8 5.5 %all-gather.3.cloned.1.call-done = bf16[256,4096]{1,0:T(8,128)(2,1)} async-done(((bf16[256,512]{1,0:T(8,128)(2,1)}), bf16[256,4096]{1,0:T(8,128)(2,1)}) %all-gather.3.cloned.1.call-update) | async-done | bytes 2097168 | tf_op jit(solution)/shard_map/all_gather | solution.py:37
  69.3 26.8 %while.2 = (s32[]{:T(128)}, bf16[256,4096]{1,0:T(8,128)(2,1)}, s32[8,2]{0,1:T(2,128)S(1)}, bf16[8,64,4096]{2,1,0:T(8,128)(2,1)}, s32[]{:T(128)}) while((s32[]{:T(128)}, bf16[256,4096]{1,0:T(8,128)(2,1)}, s32[8,2]{0,1:T(2,128)S(1)}, bf16[8,64,4096]{2,1,0:T(8,128)(2,1)}, s32[]{:T(128)}) %tuple.29), condition=%wide.while_cond, body=%wide.while_body.sunk | while | flops 2 | bytes 1049689 | solution.py:41
  69.4 0.6 slice.28
  70.0 2.7 bitcast_dynamic-update-slice_fusion.4
  72.7 0.6 slice.28
  73.3 2.7 bitcast_dynamic-update-slice_fusion.4
  76.1 0.6 slice.28
  76.7 2.8 bitcast_dynamic-update-slice_fusion.4
  79.6 0.6 slice.28
  80.2 2.7 bitcast_dynamic-update-slice_fusion.4
  82.9 0.6 slice.28
  83.5 2.7 bitcast_dynamic-update-slice_fusion.4
  86.2 0.6 slice.28
  86.8 2.7 bitcast_dynamic-update-slice_fusion.4
  89.6 0.6 slice.28
  90.2 2.7 bitcast_dynamic-update-slice_fusion.4
  92.9 0.6 slice.28
  93.5 2.6 bitcast_dynamic-update-slice_fusion.4
  96.1 107.8 %reduce-scatter.3.cloned.1.call-done = f32[896,256]{1,0:T(8,128)} async-done(((f32[7168,256]{1,0:T(8,128)}), f32[896,256]{1,0:T(8,128)}) %reduce-scatter.3.cloned.1.call-update) | async-done | bytes 917520 | tf_op jit(solution)/shard_map/reduce_scatter | solution.py:17
  203.9 1.2 convert_element_type.26
  205.1 11.4 %while.3 = (s32[]{:T(128)}, bf16[896,256]{1,0:T(8,128)(2,1)S(1)}, s32[8,2]{0,1:T(2,128)S(1)}, bf16[8,896,64]{2,1,0:T(8,128)(2,1)S(1)}, s32[]{:T(128)}) while((s32[]{:T(128)}, bf16[896,256]{1,0:T(8,128)(2,1)S(1)}, s32[8,2]{0,1:T(2,128)S(1)}, bf16[8,896,64]{2,1,0:T(8,128)(2,1)S(1)}, s32[]{:T(128)}) %tuple.32), condition=%wide.while_cond.1, body=%wide.while_body.1.sunk | while | flops 2 | bytes 458849 | solution.py:34
  205.2 0.5 slice.29
  205.7 0.8 bitcast_dynamic-update-slice_fusion.5
  206.6 0.5 slice.29
  207.1 0.8 bitcast_dynamic-update-slice_fusion.5
  208.0 0.5 slice.29
  208.6 0.8 bitcast_dynamic-update-slice_fusion.5
  209.5 0.5 slice.29
  210.0 0.8 bitcast_dynamic-update-slice_fusion.5
  210.9 0.5 slice.29
  211.4 0.8 bitcast_dynamic-update-slice_fusion.5
  212.9 0.8 bitcast_dynamic-update-slice_fusion.5
  213.8 0.5 slice.29
  214.3 0.8 bitcast_dynamic-update-slice_fusion.5
  215.2 0.5 slice.29
  215.7 0.8 bitcast_dynamic-update-slice_fusion.5
  216.5 31.8 %fusion.10 = bf16[8,32,896]{2,1,0:T(8,128)(2,1)} fusion(f32[4096,896]{1,0:T(8,128)} %param.10, bf16[8,64,4096]{2,1,0:T(8,128)(2,1)} %get-tuple-element.12, bf16[8,896,64]{2,1,0:T(8,128)(2,1)S(1)} %get-tuple-element.20, bf16[8,64]{1,0:T(8,128)(2,1)S(1)} %fusion.19, bf16[32,4096]{1,0:T(8,128)(2,1)S(1)} %all_gather.18), kind=kOutput, calls=%fused_computation.11 | convolution fusion | flops 5696552960 | bytes 20513792 | tf_op jit(solution)/shard_map/ok,skj->soj/dot_general | solution.py:48
  248.4 66.0 %all-gather.5.cloned.1.call-done = bf16[8,32,7168]{2,1,0:T(8,128)(2,1)} async-done(((bf16[8,32,896]{2,1,0:T(8,128)(2,1)}), bf16[8,32,7168]{2,1,0:T(8,128)(2,1)}) %all-gather.5.cloned.1.call-update) | async-done | bytes 3670032 | tf_op jit(solution)/shard_map/all_gather | solution.py:53
  314.4 14.2 %fusion.1 = f32[8,32,1792]{2,1,0:T(8,128)} fusion(bf16[8,32,7168]{2,1,0:T(8,128)(2,1)} %all-gather.5.cloned.1.call-done, bf16[1792,7168]{1,0:T(8,128)(2,1)} %param.9), kind=kOutput, calls=%fused_computation.6 | convolution fusion | flops 6576668672 | bytes 31195136 | tf_op jit(solution)/shard_map/sok,fk->sof/dot_general | solution.py:51
  328.6 8.0 %reduce-scatter.5.cloned.1.call-done = f32[8,32,896]{2,1,0:T(8,128)} async-done(((f32[8,32,1792]{2,1,0:T(8,128)}), f32[8,32,896]{2,1,0:T(8,128)}) %reduce-scatter.5.cloned.1.call-update) | async-done | bytes 917520 | tf_op jit(solution)/shard_map/reduce_scatter | solution.py:57
  336.6 2.0 convert_element_type.31
  (40 shorter events, 2.2 us)
Async XLA Ops:
  6.5 1.2 copy-start
  6.5 6.4 %copy-start.2 = (bf16[128,1792]{1,0:T(8,128)(2,1)S(1)}, bf16[128,1792]{1,0:T(8,128)(2,1)}, u32[]{:S(2)}) copy-start(bf16[128,1792]{1,0:T(8,128)(2,1)} %param.7) | copy-start | bytes 1376260
  6.5 62.8 %all-gather.3.cloned.1.call-start = ((), (), s32[]{:S(2)}) async-start(), calls=%async_computation.2 | async-start | bytes 2359296 | tf_op jit(solution)/shard_map/all_gather | solution.py:37
  12.9 191.0 %reduce-scatter.3.cloned.1.call-start = ((), (), s32[]{:S(2)}) async-start(), calls=%async_computation.3 | async-start | bytes 8257536 | tf_op jit(solution)/shard_map/reduce_scatter | solution.py:17
  29.3 0.7 copy-start.3
  29.3 0.9 slice-start
  29.3 285.1 %all-gather.5.cloned.1.call-start = ((), (), s32[]{:S(2)}) async-start(), calls=%async_computation.4 | async-start | bytes 4128768 | tf_op jit(solution)/shard_map/all_gather | solution.py:53
  248.3 88.3 %reduce-scatter.5.cloned.1.call-start = ((), (), s32[]{:S(2)}) async-start(), calls=%async_computation.5 | async-start | bytes 2752512 | tf_op jit(solution)/shard_map/reduce_scatter | solution.py:57
  314.4 24.3 %copy-start.1 = (bf16[128,4096]{1,0:T(8,128)(2,1)S(1)}, bf16[128,4096]{1,0:T(8,128)(2,1)}, u32[]{:S(2)}) copy-start(bf16[128,4096]{1,0:T(8,128)(2,1)} %param.6) | copy-start | bytes 3145732
Sparse Core Ops, SparseCore 0:
  13.0 56.2 all-gather.2
  72.9 130.8 reduce-scatter.2
  248.5 65.8 all-gather.4
  328.8 7.8 reduce-scatter.4
where the time goes:
time: 346 us; the launch traced here: 345 us
  waiting for transfers between devices  187 us (54%)
  matrix products  62.8 us (18%)
  local copies, waits for them, and re-layouts  39.8 us (12%)
  blocking collectives  38.2 us (11%)
  between operations  13.2 us (4%)
  other arithmetic  3.49 us (1%)
    reduce_scatter x1, waiting for transfers between devices, on_device(): lax.psum_scatter(lax.dot_general(panel, grads_all, (((0,), (1,)), ((), ()...  108 us
    all_gather x1, waiting for transfers between devices, on_device(): lax.all_gather(back_rot, 'mp', axis=2, tiled=True)  66 us
    gather x48, local copies, waits for them, and re-layouts  38 us
    all_gather x1, blocking collectives, on_device(): back_piece = lax.all_gather(rows_back, 'mp', axis=1, tiled=True)  33.6 us
    dot_general x1, matrix products, on_device(): jnp.einsum('ok,skj->soj', back_piece, scaled, preferred_element_type=jnp....  31.8 us
    dot_general x1, matrix products, on_device(): jnp.einsum('sok,fk->sof', lax.all_gather(back_rot, 'mp', axis=2, tiled=Tr...  14.2 us
    dot_general x1, matrix products, on_device(): lax.dot_general(panel, grads_all, (((0,), (1,)), ((), ())), preferred_ele...  13.8 us
    reduce_scatter x1, waiting for transfers between devices, on_device(): lax.psum_scatter(partial_out, 'dp', scatter_dimension=2, tiled=True)  8 us
  transfers between devices with their start and end apart: 4, of which 4 were waited for; matrix products, arithmetic and copies ran while one was open for 12% of the time, Pallas kernels for 0%

commit v1 on v0

v1 whole, which is shorter than its diff:
```python
import functools

import jax
import jax.numpy as jnp
from jax import lax
from jax.experimental import pallas as pl
from jax.experimental.pallas import tpu as pltpu
from jax.sharding import PartitionSpec as P

OUT_ROWS = 32
BF16 = jnp.bfloat16
F32 = jnp.float32


def fold_kernel(member, rot_in_t, rot_out_t, eigen, rows_back, out, masked, total):
    seqs = total.shape[0]
    step = pl.program_id(0)

    @pl.when(step == 0)
    def _():
        for s in range(seqs):
            masked[s] = rot_out_t[...] * member[s : s + 1, :]
        total[...] = jnp.zeros_like(total)

    inverse = 1.0 / eigen[...]
    feats = rot_in_t[...]
    rows = rows_back[...]
    for s in range(seqs):
        unscaled = lax.dot_general(
            feats, masked[s], (((1,), (1,)), ((), ())), preferred_element_type=F32
        )
        scaled = (unscaled * inverse).astype(BF16)
        total[s] += jnp.dot(rows, scaled, preferred_element_type=F32)

    @pl.when(step == pl.num_programs(0) - 1)
    def _():
        out[...] = total[...].astype(out.dtype)


def fold(member, rot_in_t, rot_out_t, eigen, rows_back, block=256):
    seqs, tokens = member.shape
    feats, cols = eigen.shape
    rows = rows_back.shape[0]
    return pl.pallas_call(
        fold_kernel,
        grid=(feats // block,),
        in_specs=[
            pl.BlockSpec((seqs, tokens), lambda k: (0, 0)),
            pl.BlockSpec((block, tokens), lambda k: (k, 0)),
            pl.BlockSpec((cols, tokens), lambda k: (0, 0)),
            pl.BlockSpec((block, cols), lambda k: (k, 0)),
            pl.BlockSpec((rows, block), lambda k: (0, k)),
        ],
        out_specs=pl.BlockSpec((seqs, rows, cols), lambda k: (0, 0, 0)),
        out_shape=jax.ShapeDtypeStruct((seqs, rows, cols), BF16),
        scratch_shapes=[
            pltpu.VMEM((seqs, cols, tokens), BF16),
            pltpu.VMEM((seqs, rows, cols), F32),
        ],
        compiler_params=pltpu.CompilerParams(vmem_limit_bytes=40 * 2**20),
        cost_estimate=pl.CostEstimate(
            flops=2 * seqs * feats * cols * (tokens + 256),
            bytes_accessed=feats * cols * 4,
            transcendentals=0,
        ),
    )(member, rot_in_t, rot_out_t, eigen, rows_back)


def on_device(acts, out_grads, basis_in, basis_out, eigen, lengths):
    rot_local = jnp.dot(acts, basis_in, preferred_element_type=F32).astype(BF16)
    rot_in = lax.all_gather(rot_local, "dp", axis=0, tiled=True)
    grads_all = lax.all_gather(out_grads, "dp", axis=0, tiled=True)
    tokens = rot_in.shape[0]
    seq_ends = jnp.cumsum(lengths)
    seq_starts = seq_ends - lengths
    position = jnp.arange(tokens, dtype=jnp.int32)
    member = (
        (position[None, :] >= seq_starts[:, None]) & (position[None, :] < seq_ends[:, None])
    ).astype(BF16)

    partial = lax.dot_general(
        basis_out, grads_all, (((0,), (1,)), ((), ())), preferred_element_type=F32
    ).astype(BF16)
    rot_out_t = lax.psum_scatter(partial, "mp", scatter_dimension=0, tiled=True)

    rot_in_t = lax.all_gather(rot_in.T, "mp", axis=0, tiled=True)
    rows_back = lax.all_gather(basis_in[:OUT_ROWS], "mp", axis=1, tiled=True)
    back_rot = fold(member, rot_in_t, rot_out_t, eigen, rows_back)
    partial_out = jnp.einsum(
        "sok,fk->sof",
        lax.all_gather(back_rot, "mp", axis=2, tiled=True),
        basis_out,
        preferred_element_type=F32,
    )
    return lax.psum_scatter(partial_out, "dp", scatter_dimension=2, tiled=True).astype(BF16)


def solution(mesh):
    placed = (
        P(("groups", "dp"), None),
        P(("groups", "dp"), "mp"),
        P(None, "mp"),
        P("mp", "dp"),
        P(None, ("dp", "mp")),
        P("groups"),
    )
    return jax.shard_map(
        on_device,
        mesh=mesh,
        in_specs=placed,
        out_specs=P("groups", None, ("mp", "dp")),
        check_vma=False,
    )
```

time: 346 us -> 302 us (0.87)
  Pallas kernels: 0 us -> 50 us
  local copies, waits for them, and re-layouts: 39.8 us -> 3.84 us
  matrix products: 62.8 us -> 31.4 us
  waiting for transfers between devices: 187 us -> 163 us
    pallas_call x0 -> x1, Pallas kernels: none -> 50 us  [fold(): pl.pallas_call(fold_kernel, grid=(feats // block,), in_specs=[pl.BlockSpe...]
    gather x48 -> x0, local copies, waits for them, and re-layouts: 38 us -> none
    dot_general x3 -> x2, matrix products: 48.5 us -> 17.2 us  [the longest x1 13.3 us: on_device(): lax.dot_general(basis_out, grads_all, (((0,), (1,)), ((), ())), preferred...]
    reduce_scatter x1, waiting for transfers between devices: 108 us -> 83.2 us  [on_device(): rot_out_t = lax.psum_scatter(partial, 'mp', scatter_dimension=0, tiled=True)]
  transfers between devices with their start and end apart: 4 -> 4, of which waited for: 4 -> 4; matrix products, arithmetic and copies ran while one was open for 12% -> 4% of each run, Pallas kernels for 0% -> 0%
where the time goes in v1:
time: 302 us
  waiting for transfers between devices  163 us (54%)
  Pallas kernels  50 us (17%)
  blocking collectives  37.9 us (13%)
  matrix products  31.4 us (10%)
  between operations  13.2 us (4%)
  local copies, waits for them, and re-layouts  3.84 us (1%)
    reduce_scatter x1, waiting for transfers between devices, on_device(): rot_out_t = lax.psum_scatter(partial, 'mp', scatter_dimension=0, tiled=True)  83.2 us
    all_gather x1, waiting for transfers between devices, on_device(): lax.all_gather(back_rot, 'mp', axis=2, tiled=True)  66.6 us
    pallas_call x1, Pallas kernels, fold(): pl.pallas_call(fold_kernel, grid=(feats // block,), in_specs=[pl.BlockSpe...  50 us
    all_gather x1, blocking collectives, on_device(): rows_back = lax.all_gather(basis_in[:OUT_ROWS], 'mp', axis=1, tiled=True)  33.3 us
    dot_general x1, matrix products, on_device(): jnp.einsum('sok,fk->sof', lax.all_gather(back_rot, 'mp', axis=2, tiled=Tr...  14.2 us
    dot_general x1, matrix products, on_device(): lax.dot_general(basis_out, grads_all, (((0,), (1,)), ((), ())), preferred...  13.3 us
    reduce_scatter x1, waiting for transfers between devices, on_device(): lax.psum_scatter(partial_out, 'dp', scatter_dimension=2, tiled=True)  8 us
  transfers between devices with their start and end apart: 4, of which 4 were waited for; matrix products, arithmetic and copies ran while one was open for 4% of the time, Pallas kernels for 0%

profile of v1, /device:TPU:0, one launch (start us, length us, event | category | flops | bytes accessed | tf_op | source)
XLA Modules:
  0.0 301.9 jit_solution(17644916984290608661)
XLA Ops:
  6.5 0.0 copy-start
  6.5 0.0 copy-start.3
  6.5 0.0 all-gather.3.cloned.1.call-start
  6.5 1.2 copy-done
  7.8 3.9 %convolution_convert_fusion.1 = bf16[128,512]{0,1:T(8,128)(2,1)S(1)} fusion(bf16[128,4096]{1,0:T(8,128)(2,1)S(1)} %copy-done, bf16[4096,512]{1,0:T(8,128)(2,1)} %param.8), kind=kOutput, calls=%fused_computation.3 | convolution fusion | flops 536936448 | bytes 5373952 | tf_op jit(solution)/shard_map/dot_general | solution.py:70
  11.7 2.2 all_gather.15
  13.9 0.0 all-gather.3.cloned.1.call-update
  13.9 0.0 reduce-scatter.3.cloned.1.call-start
  14.0 0.0 copy-done.3
  14.0 2.5 all_gather.17
  16.5 0.0 copy-start.4
  16.5 0.0 slice-start
  16.5 13.3 %convolution_convert_fusion = bf16[7168,256]{1,0:T(8,128)(2,1)} fusion(bf16[1792,7168]{1,0:T(8,128)(2,1)} %param.9, bf16[256,1792]{1,0:T(8,128)(2,1)S(1)} %all_gather.17), kind=kOutput, calls=%fused_computation.2 | convolution fusion | flops 6578503680 | bytes 30277632 | tf_op jit(solution)/shard_map/dot_general | solution.py:81
  29.7 0.0 reduce-scatter.3.cloned.1.call-update
  29.8 0.0 all-gather.5.cloned.1.call-start
  29.8 0.0 copy-done.4
  29.8 0.2 reduce-window.8
  30.0 0.0 slice-done
  30.0 33.3 %all_gather.18.rows_back = bf16[32,4096]{1,0:T(8,128)(2,1)S(1)} all-gather(bf16[32,512]{1,0:T(8,128)(2,1)S(1)} %slice-done), channel_id=1, replica_groups=mesh['groups'=2,'mp'=8,'dp'=2] {'mp'}, dimensions={1}, use_global_device_ids=true | all-gather | bytes 294912 | tf_op jit(solution)/shard_map/all_gather | solution.py:87
  63.3 0.1 fusion.3.member
  63.3 5.4 %all-gather.3.cloned.1.call-done.rot_in_t = bf16[4096,256]{1,0:T(8,128)(2,1)} async-done(((bf16[512,256]{1,0:T(8,128)(2,1)}), bf16[4096,256]{1,0:T(8,128)(2,1)}) %all-gather.3.cloned.1.call-update) | async-done | bytes 2097168 | tf_op jit(solution)/shard_map/all_gather | solution.py:86
  68.7 83.2 %reduce-scatter.3.cloned.1.call-done.rot_out_t = bf16[896,256]{1,0:T(8,128)(2,1)} async-done(((bf16[7168,256]{1,0:T(8,128)(2,1)}), bf16[896,256]{1,0:T(8,128)(2,1)}) %reduce-scatter.3.cloned.1.call-update) | async-done | bytes 458768 | tf_op jit(solution)/shard_map/reduce_scatter | solution.py:84
  151.9 0.0 copy-start.1
  151.9 1.6 copy-done.1
  153.5 0.0 copy-start.2
  153.5 1.0 copy-done.2
  154.5 50.0 %shard_map.64 = bf16[8,32,896]{2,1,0:T(8,128)(2,1)} custom-call(bf16[8,256]{1,0:T(8,128)(2,1)S(1)} %fusion.3.member, bf16[4096,256]{1,0:T(8,128)(2,1)S(1)} %copy-done.1, bf16[896,256]{1,0:T(8,128)(2,1)S(1)} %copy-done.2, f32[4096,896]{1,0:T(8,128)} %eigen.1, bf16[32,4096]{1,0:T(8,128)(2,1)S(1)} %all_gather.18.rows_back), custom_call_target="tpu_custom_call" | custom-call | flops 30064771072 | bytes 14680064 | tf_op jit(solution)/shard_map/pallas_call | solution.py:44
  204.6 0.0 all-gather.5.cloned.1.call-update
  204.6 0.0 reduce-scatter.5.cloned.1.call-start
  204.7 66.6 %all-gather.5.cloned.1.call-done = bf16[8,32,7168]{2,1,0:T(8,128)(2,1)} async-done(((bf16[8,32,896]{2,1,0:T(8,128)(2,1)}), bf16[8,32,7168]{2,1,0:T(8,128)(2,1)}) %all-gather.5.cloned.1.call-update) | async-done | bytes 3670032 | tf_op jit(solution)/shard_map/all_gather | solution.py:91
  271.2 14.2 %fusion = f32[8,32,1792]{2,1,0:T(8,128)} fusion(bf16[8,32,7168]{2,1,0:T(8,128)(2,1)} %all-gather.5.cloned.1.call-done, bf16[1792,7168]{1,0:T(8,128)(2,1)} %param.9), kind=kOutput, calls=%fused_computation | convolution fusion | flops 6576668672 | bytes 31195136 | tf_op jit(solution)/shard_map/sok,fk->sof/dot_general | solution.py:89
  285.4 0.0 reduce-scatter.5.cloned.1.call-update
  285.4 8.0 %reduce-scatter.5.cloned.1.call-done = f32[8,32,896]{2,1,0:T(8,128)} async-done(((f32[8,32,1792]{2,1,0:T(8,128)}), f32[8,32,896]{2,1,0:T(8,128)}) %reduce-scatter.5.cloned.1.call-update) | async-done | bytes 917520 | tf_op jit(solution)/shard_map/reduce_scatter | solution.py:95
  293.4 2.0 convert_element_type.15
  (1 shorter events, 0.0 us)
Async XLA Ops:
  6.5 1.2 copy-start
  6.5 7.4 %copy-start.3 = (bf16[128,1792]{1,0:T(8,128)(2,1)S(1)}, bf16[128,1792]{1,0:T(8,128)(2,1)}, u32[]{:S(2)}) copy-start(bf16[128,1792]{1,0:T(8,128)(2,1)} %param.7) | copy-start | bytes 1376260
  6.5 62.2 %all-gather.3.cloned.1.call-start = ((), (), s32[]{:S(2)}) async-start(), calls=%async_computation.2 | async-start | bytes 2359296 | tf_op jit(solution)/shard_map/all_gather | solution.py:86
  13.9 138.0 %reduce-scatter.3.cloned.1.call-start = ((), (), s32[]{:S(2)}) async-start(), calls=%async_computation.3 | async-start | bytes 4128768 | tf_op jit(solution)/shard_map/reduce_scatter | solution.py:84
  16.5 13.3 %copy-start.4 = (s32[8]{0:T(128)S(1)}, s32[8]{0:T(128)}, u32[]{:S(2)}) copy-start(s32[8]{0:T(128)} %param.11) | copy-start | bytes 100
  16.5 13.5 %slice-start = ((bf16[4096,512]{1,0:T(8,128)(2,1)}), bf16[32,512]{1,0:T(8,128)(2,1)S(1)}, s32[]{:S(2)}) async-start(bf16[4096,512]{1,0:T(8,128)(2,1)} %param.8), calls=%async_computation.6 | async-start | bytes 65536 | tf_op jit(solution)/shard_map/slice | solution.py:87
  29.8 241.5 %all-gather.5.cloned.1.call-start = ((), (), s32[]{:S(2)}) async-start(), calls=%async_computation.4 | async-start | bytes 4128768 | tf_op jit(solution)/shard_map/all_gather | solution.py:91
  151.9 1.6 copy-start.1
  153.5 1.0 copy-start.2
  204.6 88.8 %reduce-scatter.5.cloned.1.call-start = ((), (), s32[]{:S(2)}) async-start(), calls=%async_computation.5 | async-start | bytes 2752512 | tf_op jit(solution)/shard_map/reduce_scatter | solution.py:95
Sparse Core Ops, SparseCore 0:
  14.1 54.6 all-gather.2
  72.4 79.5 reduce-scatter.2
  204.7 66.4 all-gather.4
  285.5 7.8 reduce-scatter.4

commit v2 on v1

--- a/solution.py
+++ b/solution.py
@@ -10,6 +10,7 @@
 OUT_ROWS = 32
 BF16 = jnp.bfloat16
 F32 = jnp.float32
+MESH = pl.DeviceIdType.MESH
 
 
 def fold_kernel(member, rot_in_t, rot_out_t, eigen, rows_back, out, masked, total):
@@ -66,11 +67,156 @@
     )(member, rot_in_t, rot_out_t, eigen, rows_back)
 
 
+def scatter_kernel(
+    n, grads, panel, out, blocks, own, ysend, yrecv, zsend, zrecv,
+    block_sem, ys_sem, yr_sem, zs_sem, zr_sem,
+):
+    cols = out.shape[1]
+    half = n // 2
+    me = lax.axis_index("mp")
+    y, z = lax.rem(me, 2), lax.div(me, 2)
+    partner, above, below = me + 1 - 2 * y, me + 2, me - 2
+    has_above, has_below = z < half - 1, z > 0
+
+    def row(i):
+        rising = jnp.where(i < half - 1 - z, half - 1 - i, i - (half - 1 - z))
+        falling = jnp.where(i < z, i, half - 1 - (i - z))
+        return jnp.where(2 * z < half, rising, falling)
+
+    def block_copy(i, j):
+        lane = jnp.where(j == 0, 1 - y, y)
+        start = pl.multiple_of((row(i) * 2 + lane) * cols, 128)
+        return pltpu.make_async_copy(
+            panel.at[:, pl.ds(start, cols)], blocks.at[2 * i + j], block_sem.at[2 * i + j]
+        )
+
+    def y_copy(i):
+        return pltpu.make_async_remote_copy(
+            src_ref=ysend.at[i], dst_ref=yrecv.at[i], send_sem=ys_sem.at[i],
+            recv_sem=yr_sem.at[i], device_id={"mp": partner}, device_id_type=MESH,
+        )
+
+    def z_copy(i, way, target):
+        slot = row(i)
+        return pltpu.make_async_remote_copy(
+            src_ref=zsend.at[i], dst_ref=zrecv.at[way, slot], send_sem=zs_sem.at[i],
+            recv_sem=zr_sem.at[way, slot], device_id={"mp": target}, device_id_type=MESH,
+        )
+
+    for i in range(half):
+        for j in range(2):
+            block_copy(i, j).start()
+    greet(partner, above, below, has_above, has_below)
+
+    def products(i, carry):
+        block_copy(i, 0).wait()
+        ysend[i] = jnp.dot(
+            grads[...], blocks[2 * i], preferred_element_type=F32
+        ).astype(BF16)
+        y_copy(i).start()
+        block_copy(i, 1).wait()
+        own[i] = jnp.dot(grads[...], blocks[2 * i + 1], preferred_element_type=F32)
+        return carry
+
+    lax.fori_loop(0, half, products, 0)
+
+    for i in range(half):
+        y_copy(i).wait_recv()
+        own[i] += yrecv[i].astype(F32)
+        slot = row(i)
+        upward, downward = slot > z, slot < z
+        if i == half - 1:
+            upward = downward = True
+
+        @pl.when(jnp.logical_and(upward, has_below))
+        def _():
+            z_copy(i, 0, above).wait_recv()
+            own[i] += zrecv[0, slot].astype(F32)
+
+        @pl.when(jnp.logical_and(downward, has_above))
+        def _():
+            z_copy(i, 1, below).wait_recv()
+            own[i] += zrecv[1, slot].astype(F32)
+
+        if i < half - 1:
+            zsend[i] = own[i].astype(BF16)
+
+            @pl.when(upward)
+            def _():
+                z_copy(i, 0, above).start()
+
+            @pl.when(downward)
+            def _():
+                z_copy(i, 1, below).start()
+        else:
+            out[...] = own[i].astype(BF16)
+
+    for i in range(half):
+        y_copy(i).wait_send()
+        if i < half - 1:
+            z_copy(i, 0, above).wait_send()
+
+
+def greet(partner, above, below, has_above, has_below, core=None):
+    barrier = pltpu.get_barrier_semaphore()
+    pl.semaphore_signal(barrier, inc=1, device_id={"mp": partner}, device_id_type=MESH)
+    if core is not None:
+        pl.semaphore_signal(barrier, inc=1, device_id={"dp": core}, device_id_type=MESH)
+
+    @pl.when(has_above)
+    def _():
+        pl.semaphore_signal(barrier, inc=1, device_id={"mp": above}, device_id_type=MESH)
+
+    @pl.when(has_below)
+    def _():
+        pl.semaphore_signal(barrier, inc=1, device_id={"mp": below}, device_id_type=MESH)
+
+    fixed = 1 if core is None else 2
+    pl.semaphore_wait(
+        barrier, fixed + has_above.astype(jnp.int32) + has_below.astype(jnp.int32)
+    )
+
+
+def scatter_sum(n, grads, panel):
+    tokens, depth = grads.shape
+    cols = panel.shape[1] // n
+    half = n // 2
+    return pl.pallas_call(
+        functools.partial(scatter_kernel, n),
+        in_specs=[
+            pl.BlockSpec(memory_space=pltpu.VMEM),
+            pl.BlockSpec(memory_space=pl.ANY),
+        ],
+        out_specs=pl.BlockSpec(memory_space=pltpu.VMEM),
+        out_shape=jax.ShapeDtypeStruct((tokens, cols), BF16),
+        scratch_shapes=[
+            pltpu.VMEM((n, depth, cols), BF16),
+            pltpu.VMEM((half, tokens, cols), F32),
+            pltpu.VMEM((half, tokens, cols), BF16),
+            pltpu.VMEM((half, tokens, cols), BF16),
+            pltpu.VMEM((half, tokens, cols), BF16),
+            pltpu.VMEM((2, half, tokens, cols), BF16),
+            pltpu.SemaphoreType.DMA((n,)),
+            pltpu.SemaphoreType.DMA((half,)),
+            pltpu.SemaphoreType.DMA((half,)),
+            pltpu.SemaphoreType.DMA((half,)),
+            pltpu.SemaphoreType.DMA((2, half)),
+        ],
+        compiler_params=pltpu.CompilerParams(
+            collective_id=0, has_side_effects=True, vmem_limit_bytes=48 * 2**20
+        ),
+        cost_estimate=pl.CostEstimate(
+            flops=2 * tokens * depth * cols * n,
+            bytes_accessed=panel.size * 2,
+            transcendentals=0,
+        ),
+    )(grads, panel)
+
+
 def on_device(acts, out_grads, basis_in, basis_out, eigen, lengths):
     rot_local = jnp.dot(acts, basis_in, preferred_element_type=F32).astype(BF16)
-    rot_in = lax.all_gather(rot_local, "dp", axis=0, tiled=True)
     grads_all = lax.all_gather(out_grads, "dp", axis=0, tiled=True)
-    tokens = rot_in.shape[0]
+    tokens = grads_all.shape[0]
     seq_ends = jnp.cumsum(lengths)
     seq_starts = seq_ends - lengths
     position = jnp.arange(tokens, dtype=jnp.int32)
@@ -78,13 +224,19 @@
         (position[None, :] >= seq_starts[:, None]) & (position[None, :] < seq_ends[:, None])
     ).astype(BF16)
 
-    partial = lax.dot_general(
-        basis_out, grads_all, (((0,), (1,)), ((), ())), preferred_element_type=F32
-    ).astype(BF16)
-    rot_out_t = lax.psum_scatter(partial, "mp", scatter_dimension=0, tiled=True)
-
-    rot_in_t = lax.all_gather(rot_in.T, "mp", axis=0, tiled=True)
-    rows_back = lax.all_gather(basis_in[:OUT_ROWS], "mp", axis=1, tiled=True)
+    ranks = lax.axis_size("mp")
+    if ranks % 2 == 0 and eigen.shape[1] % 128 == 0:
+        rot_out_t = scatter_sum(ranks, grads_all, basis_out).T
+    else:
+        partial = lax.dot_general(
+            basis_out, grads_all, (((0,), (1,)), ((), ())), preferred_element_type=F32
+        ).astype(BF16)
+        rot_out_t = lax.psum_scatter(partial, "mp", scatter_dimension=0, tiled=True)
+
+    shared = jnp.concatenate([rot_local, basis_in[:OUT_ROWS]], axis=0)
+    shared = lax.all_gather(shared, "mp", axis=1, tiled=True)
+    rows_back = shared[rot_local.shape[0] :]
+    rot_in_t = lax.all_gather(shared[: rot_local.shape[0]], "dp", axis=0, tiled=True).T
     back_rot = fold(member, rot_in_t, rot_out_t, eigen, rows_back)
     partial_out = jnp.einsum(
         "sok,fk->sof",

time: 302 us -> 262 us (0.87)
  Pallas kernels: 50 us -> 97 us
  waiting for transfers between devices: 163 us -> 119 us
  blocking collectives: 37.9 us -> 2.46 us
  matrix products: 31.4 us -> 17.1 us
  local copies, waits for them, and re-layouts: 3.84 us -> 10.5 us
    reduce_scatter x1 -> x0, waiting for transfers between devices: 83.2 us -> none  [on_device(): rot_out_t = lax.psum_scatter(partial, 'mp', scatter_dimension=0, tiled=True)]
    pallas_call x0 -> x1, Pallas kernels: none -> 47.3 us  [scatter_sum(): pl.pallas_call(functools.partial(scatter_kernel, n), in_specs=[pl.BlockSp...]
    all_gather x1 -> x2, waiting for transfers between devices: 5.4 us -> 45.1 us  [the longest x1 45.1 us: on_device(): shared = lax.all_gather(shared, 'mp', axis=1, tiled=True)]
    all_gather x2 -> x0, blocking collectives: 35.5 us -> none  [the longest x1 33.3 us: on_device(): rows_back = lax.all_gather(basis_in[:OUT_ROWS], 'mp', axis=1, tiled=True)]
    dot_general x1 -> x0, matrix products: 13.3 us -> none  [on_device(): lax.dot_general(basis_out, grads_all, (((0,), (1,)), ((), ())), preferred...]
    transpose x0 -> x1, local copies, waits for them, and re-layouts: none -> 3.28 us  [on_device(): lax.all_gather(shared[:rot_local.shape[0]], 'dp', axis=0, tiled=True)]
    slice x2 -> x4, local copies, waits for them, and re-layouts: 0.01 us -> 3.25 us  [the longest x1 2.27 us: on_device(): shared[:rot_local.shape[0]]]
  transfers between devices with their start and end apart: 4 -> 4, of which waited for: 4 -> 3; matrix products, arithmetic and copies ran while one was open for 4% -> 1% of each run, Pallas kernels for 0% -> 18%
where the time goes in v2:
time: 262 us
  waiting for transfers between devices  119 us (45%)
  Pallas kernels  97 us (37%)
  matrix products  17.1 us (7%)
  between operations  13.2 us (5%)
  local copies, waits for them, and re-layouts  10.5 us (4%)
  other arithmetic  2.94 us (1%)
    all_gather x1, waiting for transfers between devices, on_device(): lax.all_gather(back_rot, 'mp', axis=2, tiled=True)  65.4 us
    pallas_call x1, Pallas kernels, fold(): pl.pallas_call(fold_kernel, grid=(feats // block,), in_specs=[pl.BlockSpe...  49.7 us
    pallas_call x1, Pallas kernels, scatter_sum(): pl.pallas_call(functools.partial(scatter_kernel, n), in_specs=[pl.BlockSp...  47.3 us
    all_gather x1, waiting for transfers between devices, on_device(): shared = lax.all_gather(shared, 'mp', axis=1, tiled=True)  45.1 us
    dot_general x1, matrix products, on_device(): jnp.einsum('sok,fk->sof', lax.all_gather(back_rot, 'mp', axis=2, tiled=Tr...  14.2 us
    reduce_scatter x1, waiting for transfers between devices, on_device(): lax.psum_scatter(partial_out, 'dp', scatter_dimension=2, tiled=True)  8 us
  transfers between devices with their start and end apart: 4, of which 3 were waited for; matrix products, arithmetic and copies ran while one was open for 1% of the time, Pallas kernels for 18%

profile of v2, /device:TPU:0, one launch (start us, length us, event | category | flops | bytes accessed | tf_op | source)
XLA Modules:
  0.0 261.9 jit_solution(2559462821661958239)
XLA Ops:
  6.5 0.0 copy-start
  6.5 0.0 slice-start
  6.5 0.0 all-gather.4.cloned.1.call-start
  6.5 1.2 copy-done
  7.8 0.0 copy-start.3
  7.8 3.0 %convolution_convert_fusion = bf16[128,512]{1,0:T(8,128)(2,1)S(1)} fusion(bf16[128,4096]{1,0:T(8,128)(2,1)S(1)} %copy-done, bf16[4096,512]{1,0:T(8,128)(2,1)} %param.8), kind=kOutput, calls=%fused_computation.2 | convolution fusion | flops 536936448 | bytes 5373952 | tf_op jit(solution)/shard_map/dot_general | solution.py:217
  10.7 0.0 slice-done
  10.7 0.7 pad_maximum_fusion
  11.4 0.0 all-gather.4.cloned.1.call-update
  11.4 0.0 all-gather.6.cloned.1.call-start
  11.5 45.1 %all-gather.4.cloned.1.call-done = bf16[160,4096]{1,0:T(8,128)(2,1)} async-done(((bf16[160,512]{1,0:T(8,128)(2,1)}), bf16[160,4096]{1,0:T(8,128)(2,1)}) %all-gather.4.cloned.1.call-update) | async-done | bytes 1310736 | tf_op jit(solution)/shard_map/all_gather | solution.py:237
  56.6 2.3 slice.12
  58.8 0.0 all-gather.6.cloned.1.call-update
  58.9 0.0 all-gather.8.cloned.1.call-start
  58.9 0.0 copy-done.3
  58.9 2.5 all_gather.14.grads
  61.4 0.0 copy-start.4
  61.4 47.3 %shard_map.64 = bf16[256,896]{1,0:T(8,128)(2,1)S(1)} custom-call(bf16[256,1792]{1,0:T(8,128)(2,1)S(1)} %all_gather.14.grads, bf16[1792,7168]{1,0:T(8,128)(2,1)} %panel.1), custom_call_target="tpu_custom_call" | custom-call | flops 6576668672 | bytes 25690112 | tf_op jit(solution)/shard_map/pallas_call | solution.py:184
  108.7 1.0 copy.7
  109.7 0.0 copy-done.4
  109.7 0.2 reduce-window.8
  109.9 0.1 fusion.3.member
  109.9 1.0 slice.13.rows_back
  110.9 0.0 all-gather.6.cloned.1.call-done
  110.9 3.3 %copy.8.rot_in_t = bf16[4096,256]{1,0:T(8,128)(2,1)S(1)} copy(bf16[4096,256]{0,1:T(8,128)(2,1)} %bitcast.12) | data formatting | bytes 4194304 | tf_op jit(solution)/shard_map/transpose | solution.py:239
  114.2 0.0 copy-start.1
  114.2 1.0 copy-done.1
  115.2 49.7 %shard_map.65 = bf16[8,32,896]{2,1,0:T(8,128)(2,1)S(1)} custom-call(bf16[8,256]{1,0:T(8,128)(2,1)S(1)} %fusion.3.member, bf16[4096,256]{1,0:T(8,128)(2,1)S(1)} %copy.8.rot_in_t, bf16[896,256]{1,0:T(8,128)(2,1)S(1)} %bitcast.11, f32[4096,896]{1,0:T(8,128)} %eigen.1, bf16[32,4096]{1,0:T(8,128)(2,1)S(1)} %slice.13.rows_back), custom_call_target="tpu_custom_call" | custom-call | flops 30064771072 | bytes 14680064 | tf_op jit(solution)/shard_map/pallas_call | solution.py:45
  164.9 0.0 copy-start.2
  165.0 0.8 copy-done.2
  165.7 0.0 all-gather.8.cloned.1.call-update
  165.7 0.0 reduce-scatter.2.cloned.1.call-start
  165.8 65.4 %all-gather.8.cloned.1.call-done = bf16[8,32,7168]{2,1,0:T(8,128)(2,1)} async-done(((bf16[8,32,896]{2,1,0:T(8,128)(2,1)}), bf16[8,32,7168]{2,1,0:T(8,128)(2,1)}) %all-gather.8.cloned.1.call-update) | async-done | bytes 3670032 | tf_op jit(solution)/shard_map/all_gather | solution.py:243
  231.1 14.2 %fusion = f32[8,32,1792]{2,1,0:T(8,128)} fusion(bf16[8,32,7168]{2,1,0:T(8,128)(2,1)} %all-gather.8.cloned.1.call-done, bf16[1792,7168]{1,0:T(8,128)(2,1)} %panel.1), kind=kOutput, calls=%fused_computation | convolution fusion | flops 6576668672 | bytes 31195136 | tf_op jit(solution)/shard_map/sok,fk->sof/dot_general | solution.py:241
  245.3 0.0 reduce-scatter.2.cloned.1.call-update
  245.3 8.0 %reduce-scatter.2.cloned.1.call-done = f32[8,32,896]{2,1,0:T(8,128)} async-done(((f32[8,32,1792]{2,1,0:T(8,128)}), f32[8,32,896]{2,1,0:T(8,128)}) %reduce-scatter.2.cloned.1.call-update) | async-done | bytes 917520 | tf_op jit(solution)/shard_map/reduce_scatter | solution.py:247
  253.3 2.0 convert_element_type.11
  (1 shorter events, 0.0 us)
Async XLA Ops:
  6.5 1.2 copy-start
  6.5 4.2 %slice-start = ((bf16[4096,512]{1,0:T(8,128)(2,1)}), bf16[32,512]{1,0:T(8,128)(2,1)S(1)}, s32[]{:S(2)}) async-start(bf16[4096,512]{1,0:T(8,128)(2,1)} %param.8), calls=%async_computation.5 | async-start | bytes 65536 | tf_op jit(solution)/shard_map/slice | solution.py:236
  6.5 50.0 %all-gather.4.cloned.1.call-start = ((), (), s32[]{:S(2)}) async-start(), calls=%async_computation.1 | async-start | bytes 1474560 | tf_op jit(solution)/shard_map/all_gather | solution.py:237
  7.8 51.2 %copy-start.3 = (bf16[128,1792]{1,0:T(8,128)(2,1)S(1)}, bf16[128,1792]{1,0:T(8,128)(2,1)}, u32[]{:S(2)}) copy-start(bf16[128,1792]{1,0:T(8,128)(2,1)} %param.7) | copy-start | bytes 1376260
  11.4 99.5 %all-gather.6.cloned.1.call-start = ((), (), s32[]{:S(2)}) async-start(), calls=%async_computation.2 | async-start | bytes 3145728 | tf_op jit(solution)/shard_map/all_gather | solution.py:239
  58.9 172.3 %all-gather.8.cloned.1.call-start = ((), (), s32[]{:S(2)}) async-start(), calls=%async_computation.3 | async-start | bytes 4128768 | tf_op jit(solution)/shard_map/all_gather | solution.py:243
  61.4 48.3 %copy-start.4 = (s32[8]{0:T(128)S(1)}, s32[8]{0:T(128)}, u32[]{:S(2)}) copy-start(s32[8]{0:T(128)} %param.11) | copy-start | bytes 100
  114.2 1.0 copy-start.1
  164.9 0.8 copy-start.2
  165.7 87.6 %reduce-scatter.2.cloned.1.call-start = ((), (), s32[]{:S(2)}) async-start(), calls=%async_computation.4 | async-start | bytes 2752512 | tf_op jit(solution)/shard_map/reduce_scatter | solution.py:247
Sparse Core Ops, SparseCore 0:
  11.6 44.9 all-gather.3
  59.0 9.2 all-gather.5
  165.9 65.2 all-gather.7
  245.4 7.8 reduce-scatter.1

commit v3 on v2

--- a/solution.py
+++ b/solution.py
@@ -11,60 +11,6 @@
 BF16 = jnp.bfloat16
 F32 = jnp.float32
 MESH = pl.DeviceIdType.MESH
-
-
-def fold_kernel(member, rot_in_t, rot_out_t, eigen, rows_back, out, masked, total):
-    seqs = total.shape[0]
-    step = pl.program_id(0)
-
-    @pl.when(step == 0)
-    def _():
-        for s in range(seqs):
-            masked[s] = rot_out_t[...] * member[s : s + 1, :]
-        total[...] = jnp.zeros_like(total)
-
-    inverse = 1.0 / eigen[...]
-    feats = rot_in_t[...]
-    rows = rows_back[...]
-    for s in range(seqs):
-        unscaled = lax.dot_general(
-            feats, masked[s], (((1,), (1,)), ((), ())), preferred_element_type=F32
-        )
-        scaled = (unscaled * inverse).astype(BF16)
-        total[s] += jnp.dot(rows, scaled, preferred_element_type=F32)
-
-    @pl.when(step == pl.num_programs(0) - 1)
-    def _():
-        out[...] = total[...].astype(out.dtype)
-
-
-def fold(member, rot_in_t, rot_out_t, eigen, rows_back, block=256):
-    seqs, tokens = member.shape
-    feats, cols = eigen.shape
-    rows = rows_back.shape[0]
-    return pl.pallas_call(
-        fold_kernel,
-        grid=(feats // block,),
-        in_specs=[
-            pl.BlockSpec((seqs, tokens), lambda k: (0, 0)),
-            pl.BlockSpec((block, tokens), lambda k: (k, 0)),
-            pl.BlockSpec((cols, tokens), lambda k: (0, 0)),
-            pl.BlockSpec((block, cols), lambda k: (k, 0)),
-            pl.BlockSpec((rows, block), lambda k: (0, k)),
-        ],
-        out_specs=pl.BlockSpec((seqs, rows, cols), lambda k: (0, 0, 0)),
-        out_shape=jax.ShapeDtypeStruct((seqs, rows, cols), BF16),
-        scratch_shapes=[
-            pltpu.VMEM((seqs, cols, tokens), BF16),
-            pltpu.VMEM((seqs, rows, cols), F32),
-        ],
-        compiler_params=pltpu.CompilerParams(vmem_limit_bytes=40 * 2**20),
-        cost_estimate=pl.CostEstimate(
-            flops=2 * seqs * feats * cols * (tokens + 256),
-            bytes_accessed=feats * cols * 4,
-            transcendentals=0,
-        ),
-    )(member, rot_in_t, rot_out_t, eigen, rows_back)
 
 
 def scatter_kernel(
@@ -213,34 +159,259 @@
     )(grads, panel)
 
 
+def spans(cols, width=256):
+    return [(start, min(width, cols - start)) for start in range(0, cols, width)]
+
+
+def fold_kernel(
+    n, block, member, rot_in_t, rot_out, eigen, rows_back, panel, out,
+    eig, blocks, masked, total, acc, swap, *rest,
+):
+    parts = spans(out.shape[1])
+    chunks = len(parts)
+    held = rest[:chunks]
+    eig_sem, block_sem, send_sem, recv_sem, swap_send, swap_recv = rest[chunks:]
+    feats, cols = eigen.shape
+    seqs, rows = member.shape[1], rows_back.shape[0]
+    half = n // 2
+    me, core = lax.axis_index("mp"), lax.axis_index("dp")
+    y, z = lax.rem(me, 2), lax.div(me, 2)
+    partner, above, below = me + 1 - 2 * y, me + 2, me - 2
+    has_above, has_below = z < half - 1, z > 0
+
+    def eig_copy(c):
+        start, width = parts[c]
+        span = pl.ds(start, width)
+        return pltpu.make_async_copy(eigen.at[:, span], eig.at[:, span], eig_sem.at[c])
+
+    def block_copy(d):
+        start = pl.multiple_of(d * cols, 128)
+        return pltpu.make_async_copy(
+            panel.at[:, pl.ds(start, cols)], blocks.at[d], block_sem.at[d]
+        )
+
+    def pass_on(c, place, kind):
+        slot = place * 2 + y
+        return pltpu.make_async_remote_copy(
+            src_ref=held[c].at[slot], dst_ref=held[c].at[slot],
+            send_sem=send_sem.at[c, place, kind], recv_sem=recv_sem.at[c, slot],
+            device_id={"mp": (partner, above, below)[kind]}, device_id_type=MESH,
+        )
+
+    def arrived(c, slot):
+        pltpu.make_async_remote_copy(
+            src_ref=held[c].at[slot], dst_ref=held[c].at[slot],
+            send_sem=send_sem.at[c, 0, 0], recv_sem=recv_sem.at[c, slot],
+            device_id={"mp": partner}, device_id_type=MESH,
+        ).wait_recv()
+
+    def send_own(c):
+        @pl.when(has_above)
+        def _():
+            pass_on(c, z, 1).start()
+
+        @pl.when(has_below)
+        def _():
+            pass_on(c, z, 2).start()
+
+        pass_on(c, z, 0).start()
+
+    def hop(c, h):
+        @pl.when(z - h >= 0)
+        def _():
+            arrived(c, (z - h) * 2 + y)
+
+            @pl.when(has_above)
+            def _():
+                pass_on(c, z - h, 1).start()
+
+            pass_on(c, z - h, 0).start()
+
+        @pl.when(z + h <= half - 1)
+        def _():
+            arrived(c, (z + h) * 2 + y)
+
+            @pl.when(has_below)
+            def _():
+                pass_on(c, z + h, 2).start()
+
+            pass_on(c, z + h, 0).start()
+
+    def events(unit):
+        for c in range(chunks):
+            h = unit - 2 * (c + 1)
+            if h == 0:
+                send_own(c)
+            elif 0 < h < half:
+                hop(c, h)
+
+    def fold_part(c, low, high):
+        start, width = parts[c]
+
+        def body(k, carry):
+            at = pl.ds(pl.multiple_of(k * block, block), block)
+            inverse = 1.0 / eig[at, start : start + width]
+            unscaled = jnp.dot(
+                rot_in_t[at, :], masked[:, : seqs * width], preferred_element_type=F32
+            )
+            scaled = (unscaled * jnp.concatenate([inverse] * seqs, axis=1)).astype(BF16)
+            total[:, : seqs * width] += jnp.dot(
+                rows_back[:, at], scaled, preferred_element_type=F32
+            )
+            return carry
+
+        lax.fori_loop(low, high, body, 0)
+
+    def project(c, low, high, part, wait):
+        start, width = parts[c]
+        at = pl.ds(pl.multiple_of(part * cols, 128), cols)
+
+        def body(d, carry):
+            if wait:
+
+                @pl.when(lax.rem(d, 2) != y)
+                def _():
+                    arrived(c, d)
+
+            acc[part] += lax.dot_general(
+                held[c][d], blocks[d, at, start : start + width],
+                (((1,), (1,)), ((), ())), preferred_element_type=F32,
+            )
+            return carry
+
+        lax.fori_loop(low, high, body, 0)
+
+    for c in range(chunks):
+        eig_copy(c).start()
+    for d in range(n):
+        block_copy(d).start()
+    greet(partner, above, below, has_above, has_below, 1 - core)
+
+    steps = feats // block
+    for c, (start, width) in enumerate(parts):
+        for s in range(seqs):
+            masked[:, s * width : (s + 1) * width] = (
+                rot_out[:, start : start + width] * member[:, s : s + 1]
+            )
+        total[...] = jnp.zeros_like(total)
+        eig_copy(c).wait()
+        fold_part(c, 0, steps // 2)
+        events(2 * c + 1)
+        fold_part(c, steps // 2, steps)
+        for s in range(seqs):
+            held[c][me, s * rows : (s + 1) * rows, :] = total[
+                :, s * width : (s + 1) * width
+            ].astype(BF16)
+        events(2 * c + 2)
+
+    for d in range(n):
+        block_copy(d).wait()
+    acc[...] = jnp.zeros_like(acc)
+    unit = 2 * chunks
+    for c in range(chunks - 1):
+        for low, high in ((0, half), (half, n)):
+            project(c, low, high, 0, True)
+            project(c, low, high, 1, False)
+            unit += 1
+            events(unit)
+    last = chunks - 1
+    for later in range(unit + 1, 2 * chunks + half):
+        events(later)
+    project(last, 0, n, 1 - core, True)
+    exchange = pltpu.make_async_remote_copy(
+        src_ref=acc.at[1 - core], dst_ref=swap, send_sem=swap_send, recv_sem=swap_recv,
+        device_id={"dp": 1 - core}, device_id_type=MESH,
+    )
+    exchange.start()
+    project(last, 0, n, core, False)
+    exchange.wait()
+    out[...] = (acc[core] + swap[...]).astype(BF16)
+
+    for c in range(chunks):
+        for place in range(half):
+            pass_on(c, place, 0).wait_send()
+
+            @pl.when(jnp.logical_and(place <= z, has_above))
+            def _():
+                pass_on(c, place, 1).wait_send()
+
+            @pl.when(jnp.logical_and(place >= z, has_below))
+            def _():
+                pass_on(c, place, 2).wait_send()
+
+
+def fold_and_project(n, member, rot_in_t, rot_out, eigen, rows_back, panel, block=512):
+    tokens, seqs = member.shape
+    feats, cols = eigen.shape
+    rows, depth = rows_back.shape[0], panel.shape[0]
+    parts = spans(cols)
+    widest = max(width for _, width in parts)
+    vmem = pl.BlockSpec(memory_space=pltpu.VMEM)
+    hbm = pl.BlockSpec(memory_space=pl.ANY)
+    return pl.pallas_call(
+        functools.partial(fold_kernel, n, block),
+        in_specs=[vmem, vmem, vmem, hbm, vmem, hbm],
+        out_specs=vmem,
+        out_shape=jax.ShapeDtypeStruct((seqs * rows, cols), BF16),
+        scratch_shapes=[
+            pltpu.VMEM((feats, cols), F32),
+            pltpu.VMEM((n, depth, cols), BF16),
+            pltpu.VMEM((tokens, seqs * widest), BF16),
+            pltpu.VMEM((rows, seqs * widest), F32),
+            pltpu.VMEM((2, seqs * rows, cols), F32),
+            pltpu.VMEM((seqs * rows, cols), F32),
+            *[pltpu.VMEM((n, seqs * rows, width), BF16) for _, width in parts],
+            pltpu.SemaphoreType.DMA((len(parts),)),
+            pltpu.SemaphoreType.DMA((n,)),
+            pltpu.SemaphoreType.DMA((len(parts), n // 2, 3)),
+            pltpu.SemaphoreType.DMA((len(parts), n)),
+            pltpu.SemaphoreType.DMA,
+            pltpu.SemaphoreType.DMA,
+        ],
+        compiler_params=pltpu.CompilerParams(
+            collective_id=1, has_side_effects=True, vmem_limit_bytes=61 * 2**20
+        ),
+        cost_estimate=pl.CostEstimate(
+            flops=2 * seqs * feats * cols * (tokens + 256),
+            bytes_accessed=feats * cols * 4 + panel.size * 2,
+            transcendentals=0,
+        ),
+    )(member, rot_in_t, rot_out, eigen, rows_back, panel)
+
+
 def on_device(acts, out_grads, basis_in, basis_out, eigen, lengths):
+    ranks = lax.axis_size("mp")
+    cols = eigen.shape[1]
     rot_local = jnp.dot(acts, basis_in, preferred_element_type=F32).astype(BF16)
     grads_all = lax.all_gather(out_grads, "dp", axis=0, tiled=True)
-    tokens = grads_all.shape[0]
-    seq_ends = jnp.cumsum(lengths)
-    seq_starts = seq_ends - lengths
-    position = jnp.arange(tokens, dtype=jnp.int32)
-    member = (
-        (position[None, :] >= seq_starts[:, None]) & (position[None, :] < seq_ends[:, None])
-    ).astype(BF16)
-
-    ranks = lax.axis_size("mp")
-    if ranks % 2 == 0 and eigen.shape[1] % 128 == 0:
-        rot_out_t = scatter_sum(ranks, grads_all, basis_out).T
-    else:
-        partial = lax.dot_general(
-            basis_out, grads_all, (((0,), (1,)), ((), ())), preferred_element_type=F32
-        ).astype(BF16)
-        rot_out_t = lax.psum_scatter(partial, "mp", scatter_dimension=0, tiled=True)
-
+    tokens, seqs = grads_all.shape[0], lengths.shape[0]
     shared = jnp.concatenate([rot_local, basis_in[:OUT_ROWS]], axis=0)
     shared = lax.all_gather(shared, "mp", axis=1, tiled=True)
     rows_back = shared[rot_local.shape[0] :]
-    rot_in_t = lax.all_gather(shared[: rot_local.shape[0]], "dp", axis=0, tiled=True).T
-    back_rot = fold(member, rot_in_t, rot_out_t, eigen, rows_back)
+    rot_in = lax.all_gather(shared[: rot_local.shape[0]], "dp", axis=0, tiled=True)
+    seq_ends = jnp.cumsum(lengths)
+    seq_starts = seq_ends - lengths
+    position = jnp.arange(tokens, dtype=jnp.int32)[:, None]
+    member = ((position >= seq_starts) & (position < seq_ends)).astype(BF16)
+
+    if ranks % 2 == 0 and 4 <= ranks <= 8 and cols % 128 == 0:
+        rot_out = scatter_sum(ranks, grads_all, basis_out)
+        result = fold_and_project(
+            ranks, member, rot_in.T, rot_out, eigen, rows_back, basis_out
+        )
+        return result.reshape(seqs, OUT_ROWS, cols)
+
+    partial = lax.dot_general(
+        basis_out, grads_all, (((0,), (1,)), ((), ())), preferred_element_type=F32
+    )
+    rot_out = lax.psum_scatter(partial, "mp", scatter_dimension=0, tiled=True).astype(BF16)
+    masked = rot_out[None, :, :] * member.T[:, None, :]
+    unscaled = jnp.einsum("tk,sjt->skj", rot_in, masked, preferred_element_type=F32)
+    scaled = (unscaled / eigen[None, :, :]).astype(BF16)
+    back_rot = jnp.einsum("ok,skj->soj", rows_back, scaled, preferred_element_type=F32)
     partial_out = jnp.einsum(
         "sok,fk->sof",
-        lax.all_gather(back_rot, "mp", axis=2, tiled=True),
+        lax.all_gather(back_rot.astype(BF16), "mp", axis=2, tiled=True),
         basis_out,
         preferred_element_type=F32,
     )

time: 262 us -> 193 us (0.74)
  waiting for transfers between devices: 119 us -> 45.1 us
  Pallas kernels: 97 us -> 116 us
  matrix products: 17.1 us -> 2.96 us
    all_gather x1 -> x0, waiting for transfers between devices: 65.4 us -> none  [on_device(): lax.all_gather(back_rot, 'mp', axis=2, tiled=True)]
    pallas_call x1, Pallas kernels: 49.7 us -> 68.4 us  [fold_and_project(): pl.pallas_call(functools.partial(fold_kernel, n, block), in_specs=[vmem,...]
    dot_general x1 -> x0, matrix products: 14.2 us -> none  [on_device(): jnp.einsum('sok,fk->sof', lax.all_gather(back_rot, 'mp', axis=2, tiled=Tr...]
    reduce_scatter x1 -> x0, waiting for transfers between devices: 8 us -> none  [on_device(): lax.psum_scatter(partial_out, 'dp', scatter_dimension=2, tiled=True)]
  transfers between devices with their start and end apart: 4 -> 2, of which waited for: 3 -> 1; matrix products, arithmetic and copies ran while one was open for 1% -> 1% of each run, Pallas kernels for 18% -> 24%
where the time goes in v3:
time: 193 us
  Pallas kernels  116 us (60%)
  waiting for transfers between devices  45.1 us (23%)
  between operations  13.5 us (7%)
  local copies, waits for them, and re-layouts  11.8 us (6%)
  matrix products  2.96 us (2%)
  blocking collectives  2.45 us (1%)
    pallas_call x1, Pallas kernels, fold_and_project(): pl.pallas_call(functools.partial(fold_kernel, n, block), in_specs=[vmem,...  68.4 us
    pallas_call x1, Pallas kernels, scatter_sum(): pl.pallas_call(functools.partial(scatter_kernel, n), in_specs=[pl.BlockSp...  47.2 us
    all_gather x1, waiting for transfers between devices, on_device(): shared = lax.all_gather(shared, 'mp', axis=1, tiled=True)  45.1 us
    transpose x1, local copies, waits for them, and re-layouts, on_device(): result = fold_and_project(ranks, member, rot_in.T, rot_out, eigen, rows_b...  4.06 us
  transfers between devices with their start and end apart: 2, of which 1 were waited for; matrix products, arithmetic and copies ran while one was open for 1% of the time, Pallas kernels for 24%

profile of v3, /device:TPU:0, one launch (start us, length us, event | category | flops | bytes accessed | tf_op | source)
XLA Modules:
  0.0 193.0 jit_solution(98370030732048761)
XLA Ops:
  6.5 0.0 copy-start
  6.5 0.0 slice-start
  6.5 0.0 all-gather.3.cloned.1.call-start
  6.5 1.2 copy-done
  7.8 0.0 copy-start.3
  7.8 0.0 copy-start.2
  7.8 3.0 %convolution_convert_fusion = bf16[128,512]{1,0:T(8,128)(2,1)S(1)} fusion(bf16[128,4096]{1,0:T(8,128)(2,1)S(1)} %copy-done, bf16[4096,512]{1,0:T(8,128)(2,1)} %param.8), kind=kOutput, calls=%fused_computation | convolution fusion | flops 536936448 | bytes 5373952 | tf_op jit(solution)/shard_map/dot_general | solution.py:385
  10.7 0.0 slice-done
  10.7 0.7 pad_maximum_fusion
  11.4 0.0 all-gather.3.cloned.1.call-update
  11.4 0.0 all-gather.5.cloned.1.call-start
  11.5 45.1 %all-gather.3.cloned.1.call-done = bf16[160,4096]{1,0:T(8,128)(2,1)} async-done(((bf16[160,512]{1,0:T(8,128)(2,1)}), bf16[160,4096]{1,0:T(8,128)(2,1)}) %all-gather.3.cloned.1.call-update) | async-done | bytes 1310736 | tf_op jit(solution)/shard_map/all_gather | solution.py:389
  56.6 2.3 %slice.12 = bf16[128,4096]{1,0:T(8,128)(2,1)} slice(bf16[160,4096]{1,0:T(8,128)(2,1)} %all-gather.3.cloned.1.call-done), slice={[0:128], [0:4096]} | slice | bytes 2097152 | tf_op jit(solution)/shard_map/slice | solution.py:391
  58.8 0.0 all-gather.5.cloned.1.call-update
  58.9 0.0 copy-done.3
  58.9 0.2 reduce-window.8
  59.1 0.6 fusion.1.member
  59.7 0.0 copy-done.2
  59.7 2.5 %all_gather.11.grads = bf16[256,1792]{1,0:T(8,128)(2,1)S(1)} all-gather(bf16[128,1792]{1,0:T(8,128)(2,1)S(1)} %copy-done.2), channel_id=1, replica_groups=mesh['groups'=2,'mp'=8,'dp'=2] {'dp'}, dimensions={0}, use_global_device_ids=true | all-gather | bytes 1376256 | tf_op jit(solution)/shard_map/all_gather | solution.py:386
  62.2 47.2 %shard_map.64.rot_out = bf16[256,896]{1,0:T(8,128)(2,1)S(1)} custom-call(bf16[256,1792]{1,0:T(8,128)(2,1)S(1)} %all_gather.11.grads, bf16[1792,7168]{1,0:T(8,128)(2,1)} %panel.3), custom_call_target="tpu_custom_call" | custom-call | flops 6576668672 | bytes 25690112 | tf_op jit(solution)/shard_map/pallas_call | solution.py:130
  109.4 0.0 copy-start.1
  109.4 0.8 copy-done.1
  110.2 1.7 slice.13.rows_back
  111.8 0.0 all-gather.5.cloned.1.call-done
  111.8 4.1 %copy.9.rot_in_t = bf16[4096,256]{1,0:T(8,128)(2,1)} copy(bf16[4096,256]{0,1:T(8,128)(2,1)} %bitcast.7) | data formatting | bytes 4194304 | tf_op jit(solution)/shard_map/transpose | solution.py:400
  115.9 68.4 %shard_map.65 = bf16[256,896]{1,0:T(8,128)(2,1)} custom-call(bf16[256,8]{1,0:T(8,128)(2,1)} %fusion.1.member, bf16[4096,256]{1,0:T(8,128)(2,1)} %copy.9.rot_in_t, bf16[256,896]{1,0:T(8,128)(2,1)} %copy-done.1, f32[4096,896]{1,0:T(8,128)} %eigen.1, bf16[32,4096]{1,0:T(8,128)(2,1)} %slice.13.rows_back, bf16[1792,7168]{1,0:T(8,128)(2,1)} %panel.3), custom_call_target="tpu_custom_call" | custom-call | flops 30064771072 | bytes 40370176 | tf_op jit(solution)/shard_map/pallas_call | solution.py:351
  184.3 1.8 copy.11
  (1 shorter events, 0.0 us)
Async XLA Ops:
  6.5 1.2 copy-start
  6.5 4.2 %slice-start = ((bf16[4096,512]{1,0:T(8,128)(2,1)}), bf16[32,512]{1,0:T(8,128)(2,1)S(1)}, s32[]{:S(2)}) async-start(bf16[4096,512]{1,0:T(8,128)(2,1)} %param.8), calls=%async_computation.2 | async-start | bytes 65536 | tf_op jit(solution)/shard_map/slice | solution.py:388
  6.5 50.0 %all-gather.3.cloned.1.call-start = ((), (), s32[]{:S(2)}) async-start(), calls=%async_computation | async-start | bytes 1474560 | tf_op jit(solution)/shard_map/all_gather | solution.py:389
  7.8 51.1 %copy-start.3 = (s32[8]{0:T(128)S(1)}, s32[8]{0:T(128)}, u32[]{:S(2)}) copy-start(s32[8]{0:T(128)} %param.11) | copy-start | bytes 100
  7.8 52.0 %copy-start.2 = (bf16[128,1792]{1,0:T(8,128)(2,1)S(1)}, bf16[128,1792]{1,0:T(8,128)(2,1)}, u32[]{:S(2)}) copy-start(bf16[128,1792]{1,0:T(8,128)(2,1)} %param.7) | copy-start | bytes 1376260
  11.4 100.4 %all-gather.5.cloned.1.call-start = ((), (), s32[]{:S(2)}) async-start(), calls=%async_computation.1 | async-start | bytes 3145728 | tf_op jit(solution)/shard_map/all_gather | solution.py:391
  109.4 0.8 copy-start.1
Sparse Core Ops, SparseCore 0:
  11.6 44.9 all-gather.2
  59.0 9.2 all-gather.4

commit v4 on v3

--- a/solution.py
+++ b/solution.py
@@ -14,12 +14,14 @@
 
 
 def scatter_kernel(
-    n, grads, panel, out, blocks, own, ysend, yrecv, zsend, zrecv,
-    block_sem, ys_sem, yr_sem, zs_sem, zr_sem,
+    n, grads_own, feat_t, rows, panel, out, shared, grads, blocks, own, ysend, yrecv,
+    zsend, zrecv, block_sem, ys_sem, yr_sem, zs_sem, zr_sem, fs_sem, fr_sem, fc_sem,
+    grads_sem,
 ):
     cols = out.shape[1]
+    feats, tokens = feat_t.shape
     half = n // 2
-    me = lax.axis_index("mp")
+    me, core = lax.axis_index("mp"), lax.axis_index("dp")
     y, z = lax.rem(me, 2), lax.div(me, 2)
     partner, above, below = me + 1 - 2 * y, me + 2, me - 2
     has_above, has_below = z < half - 1, z > 0
@@ -49,12 +51,75 @@
             recv_sem=zr_sem.at[way, slot], device_id={"mp": target}, device_id_type=MESH,
         )
 
+    lanes = pl.ds(pl.multiple_of(core * tokens, 128), tokens)
+    their_lanes = pl.ds(pl.multiple_of((1 - core) * tokens, 128), tokens)
+    own_rows = pl.ds(pl.multiple_of(core * tokens, 16), tokens)
+
+    def item_copy(slot, kind):
+        block = shared.at[slot, :, lanes]
+        if kind == 3:
+            return pltpu.make_async_remote_copy(
+                src_ref=block, dst_ref=block, send_sem=fs_sem.at[slot, 3],
+                recv_sem=fc_sem.at[slot], device_id={"dp": 1 - core}, device_id_type=MESH,
+            )
+        return pltpu.make_async_remote_copy(
+            src_ref=block, dst_ref=block, send_sem=fs_sem.at[slot, kind],
+            recv_sem=fr_sem.at[slot], device_id={"mp": (partner, above, below)[kind]},
+            device_id_type=MESH,
+        )
+
+    def onward(slot, up, down):
+        if up:
+
+            @pl.when(has_above)
+            def _():
+                item_copy(slot, 1).start()
+
+        if down:
+
+            @pl.when(has_below)
+            def _():
+                item_copy(slot, 2).start()
+
+        item_copy(slot, 3).start()
+
+    def item_hop(h):
+        for lane in range(2):
+
+            @pl.when(z - h >= 0)
+            def _():
+                slot = (z - h) * 2 + lane
+                item_copy(slot, 0).wait_recv()
+                onward(slot, True, False)
+
+            @pl.when(z + h <= half - 1)
+            def _():
+                slot = (z + h) * 2 + lane
+                item_copy(slot, 0).wait_recv()
+                onward(slot, False, True)
+
     for i in range(half):
         for j in range(2):
             block_copy(i, j).start()
-    greet(partner, above, below, has_above, has_below)
-
-    def products(i, carry):
+    shared[me, :feats, lanes] = feat_t[...]
+    share = rows.shape[0] // 2
+    for q in range(feats // 128):
+        shared[me, feats + q * share : feats + (q + 1) * share, lanes] = rows[
+            pl.ds(pl.multiple_of(core * share, 16), share), q * 128 : (q + 1) * 128
+        ]
+    grads[own_rows, :] = grads_own[...]
+    greet(partner, above, below, has_above, has_below, 1 - core)
+    grads_copy = pltpu.make_async_remote_copy(
+        src_ref=grads.at[own_rows], dst_ref=grads.at[own_rows],
+        send_sem=grads_sem.at[0], recv_sem=grads_sem.at[1],
+        device_id={"dp": 1 - core}, device_id_type=MESH,
+    )
+    grads_copy.start()
+    item_copy(me, 0).start()
+    onward(me, True, True)
+    grads_copy.wait_recv()
+
+    def products(i):
         block_copy(i, 0).wait()
         ysend[i] = jnp.dot(
             grads[...], blocks[2 * i], preferred_element_type=F32
@@ -62,9 +127,14 @@
         y_copy(i).start()
         block_copy(i, 1).wait()
         own[i] = jnp.dot(grads[...], blocks[2 * i + 1], preferred_element_type=F32)
-        return carry
-
-    lax.fori_loop(0, half, products, 0)
+
+    for i in range(half):
+        products(i)
+        if i == 0:
+            item_copy(partner, 0).wait_recv()
+            onward(partner, True, True)
+        else:
+            item_hop(i)
 
     for i in range(half):
         y_copy(i).wait_recv()
@@ -102,6 +172,25 @@
         if i < half - 1:
             z_copy(i, 0, above).wait_send()
 
+    grads_copy.wait_send()
+    item_copy(me, 0).wait_send()
+    for slot in range(n):
+        item_copy(slot, 3).wait_send()
+
+        @pl.when(jnp.logical_and(slot // 2 <= z, has_above))
+        def _():
+            item_copy(slot, 1).wait_send()
+
+        @pl.when(jnp.logical_and(slot // 2 >= z, has_below))
+        def _():
+            item_copy(slot, 2).wait_send()
+
+        pltpu.make_async_remote_copy(
+            src_ref=shared.at[slot, :, their_lanes], dst_ref=shared.at[slot, :, their_lanes],
+            send_sem=fs_sem.at[slot, 3], recv_sem=fc_sem.at[slot],
+            device_id={"dp": 1 - core}, device_id_type=MESH,
+        ).wait_recv()
+
 
 def greet(partner, above, below, has_above, has_below, core=None):
     barrier = pltpu.get_barrier_semaphore()
@@ -123,19 +212,27 @@
     )
 
 
-def scatter_sum(n, grads, panel):
-    tokens, depth = grads.shape
+def scatter_sum(n, grads, feat_t, rows, panel):
+    tokens, depth = 2 * grads.shape[0], grads.shape[1]
+    feats = feat_t.shape[0]
+    extra = rows.shape[0] // 2 * (feats // 128)
     cols = panel.shape[1] // n
     half = n // 2
     return pl.pallas_call(
         functools.partial(scatter_kernel, n),
         in_specs=[
             pl.BlockSpec(memory_space=pltpu.VMEM),
+            pl.BlockSpec(memory_space=pltpu.VMEM),
+            pl.BlockSpec(memory_space=pltpu.VMEM),
             pl.BlockSpec(memory_space=pl.ANY),
         ],
-        out_specs=pl.BlockSpec(memory_space=pltpu.VMEM),
-        out_shape=jax.ShapeDtypeStruct((tokens, cols), BF16),
+        out_specs=[pl.BlockSpec(memory_space=pltpu.VMEM)] * 2,
+        out_shape=[
+            jax.ShapeDtypeStruct((tokens, cols), BF16),
+            jax.ShapeDtypeStruct((n, feats + extra, tokens), BF16),
+        ],
         scratch_shapes=[
+            pltpu.VMEM((tokens, depth), BF16),
             pltpu.VMEM((n, depth, cols), BF16),
             pltpu.VMEM((half, tokens, cols), F32),
             pltpu.VMEM((half, tokens, cols), BF16),
@@ -147,6 +244,10 @@
             pltpu.SemaphoreType.DMA((half,)),
             pltpu.SemaphoreType.DMA((half,)),
             pltpu.SemaphoreType.DMA((2, half)),
+            pltpu.SemaphoreType.DMA((n, 4)),
+            pltpu.SemaphoreType.DMA((n,)),
+            pltpu.SemaphoreType.DMA((n,)),
+            pltpu.SemaphoreType.DMA((2,)),
         ],
         compiler_params=pltpu.CompilerParams(
             collective_id=0, has_side_effects=True, vmem_limit_bytes=48 * 2**20
@@ -156,7 +257,7 @@
             bytes_accessed=panel.size * 2,
             transcendentals=0,
         ),
-    )(grads, panel)
+    )(grads, feat_t, rows, panel)
 
 
 def spans(cols, width=256):
@@ -164,8 +265,8 @@
 
 
 def fold_kernel(
-    n, block, member, rot_in_t, rot_out, eigen, rows_back, panel, out,
-    eig, blocks, masked, total, acc, swap, *rest,
+    n, member, shared, rot_out, eigen, panel, out,
+    eig, blocks, masked, total, acc, swap, rows_back, *rest,
 ):
     parts = spans(out.shape[1])
     chunks = len(parts)
@@ -174,6 +275,7 @@
     feats, cols = eigen.shape
     seqs, rows = member.shape[1], rows_back.shape[0]
     half = n // 2
+    block, share = feats // n, rows // 2
     me, core = lax.axis_index("mp"), lax.axis_index("dp")
     y, z = lax.rem(me, 2), lax.div(me, 2)
     partner, above, below = me + 1 - 2 * y, me + 2, me - 2
@@ -252,7 +354,7 @@
             at = pl.ds(pl.multiple_of(k * block, block), block)
             inverse = 1.0 / eig[at, start : start + width]
             unscaled = jnp.dot(
-                rot_in_t[at, :], masked[:, : seqs * width], preferred_element_type=F32
+                shared[k, :block, :], masked[:, : seqs * width], preferred_element_type=F32
             )
             scaled = (unscaled * jnp.concatenate([inverse] * seqs, axis=1)).astype(BF16)
             total[:, : seqs * width] += jnp.dot(
@@ -285,6 +387,14 @@
         eig_copy(c).start()
     for d in range(n):
         block_copy(d).start()
+    for d in range(n):
+        for half_row in range(2):
+            for q in range(block // 128):
+                at = block + q * share
+                rows_back[
+                    half_row * share : (half_row + 1) * share,
+                    d * block + q * 128 : d * block + (q + 1) * 128,
+                ] = shared[d, at : at + share, half_row * 128 : (half_row + 1) * 128]
     greet(partner, above, below, has_above, has_below, 1 - core)
 
     steps = feats // block
@@ -340,17 +450,17 @@
                 pass_on(c, place, 2).wait_send()
 
 
-def fold_and_project(n, member, rot_in_t, rot_out, eigen, rows_back, panel, block=512):
+def fold_and_project(n, member, shared, rot_out, eigen, rows, panel):
     tokens, seqs = member.shape
     feats, cols = eigen.shape
-    rows, depth = rows_back.shape[0], panel.shape[0]
+    depth = panel.shape[0]
     parts = spans(cols)
     widest = max(width for _, width in parts)
     vmem = pl.BlockSpec(memory_space=pltpu.VMEM)
     hbm = pl.BlockSpec(memory_space=pl.ANY)
     return pl.pallas_call(
-        functools.partial(fold_kernel, n, block),
-        in_specs=[vmem, vmem, vmem, hbm, vmem, hbm],
+        functools.partial(fold_kernel, n),
+        in_specs=[vmem, vmem, vmem, hbm, hbm],
         out_specs=vmem,
         out_shape=jax.ShapeDtypeStruct((seqs * rows, cols), BF16),
         scratch_shapes=[
@@ -360,6 +470,7 @@
             pltpu.VMEM((rows, seqs * widest), F32),
             pltpu.VMEM((2, seqs * rows, cols), F32),
             pltpu.VMEM((seqs * rows, cols), F32),
+            pltpu.VMEM((rows, feats), BF16),
             *[pltpu.VMEM((n, seqs * rows, width), BF16) for _, width in parts],
             pltpu.SemaphoreType.DMA((len(parts),)),
             pltpu.SemaphoreType.DMA((n,)),
@@ -376,31 +487,39 @@
             bytes_accessed=feats * cols * 4 + panel.size * 2,
             transcendentals=0,
         ),
-    )(member, rot_in_t, rot_out, eigen, rows_back, panel)
+    )(member, shared, rot_out, eigen, panel)
 
 
 def on_device(acts, out_grads, basis_in, basis_out, eigen, lengths):
     ranks = lax.axis_size("mp")
     cols = eigen.shape[1]
-    rot_local = jnp.dot(acts, basis_in, preferred_element_type=F32).astype(BF16)
-    grads_all = lax.all_gather(out_grads, "dp", axis=0, tiled=True)
-    tokens, seqs = grads_all.shape[0], lengths.shape[0]
-    shared = jnp.concatenate([rot_local, basis_in[:OUT_ROWS]], axis=0)
-    shared = lax.all_gather(shared, "mp", axis=1, tiled=True)
-    rows_back = shared[rot_local.shape[0] :]
-    rot_in = lax.all_gather(shared[: rot_local.shape[0]], "dp", axis=0, tiled=True)
+    tokens, seqs = 2 * out_grads.shape[0], lengths.shape[0]
     seq_ends = jnp.cumsum(lengths)
     seq_starts = seq_ends - lengths
     position = jnp.arange(tokens, dtype=jnp.int32)[:, None]
     member = ((position >= seq_starts) & (position < seq_ends)).astype(BF16)
-
-    if ranks % 2 == 0 and 4 <= ranks <= 8 and cols % 128 == 0:
-        rot_out = scatter_sum(ranks, grads_all, basis_out)
+    rows = basis_in[:OUT_ROWS]
+
+    if (
+        ranks in (4, 8)
+        and cols % 128 == 0
+        and basis_in.shape[1] % 128 == 0
+        and acts.shape[0] == 128
+    ):
+        feat_t = lax.dot_general(
+            basis_in, acts, (((0,), (1,)), ((), ())), preferred_element_type=F32
+        ).astype(BF16)
+        rot_out, shared = scatter_sum(ranks, out_grads, feat_t, rows, basis_out)
         result = fold_and_project(
-            ranks, member, rot_in.T, rot_out, eigen, rows_back, basis_out
+            ranks, member, shared, rot_out, eigen, OUT_ROWS, basis_out
         )
         return result.reshape(seqs, OUT_ROWS, cols)
 
+    rot_local = jnp.dot(acts, basis_in, preferred_element_type=F32).astype(BF16)
+    grads_all = lax.all_gather(out_grads, "dp", axis=0, tiled=True)
+    shared = lax.all_gather(jnp.concatenate([rot_local, rows], axis=0), "mp", axis=1, tiled=True)
+    rows_back = shared[rot_local.shape[0] :]
+    rot_in = lax.all_gather(shared[: rot_local.shape[0]], "dp", axis=0, tiled=True)
     partial = lax.dot_general(
         basis_out, grads_all, (((0,), (1,)), ((), ())), preferred_element_type=F32
     )

time: 193 us -> 137 us (0.71)
  waiting for transfers between devices: 45.1 us -> 0 us
  between operations: 13.5 us -> 0.04 us
  Pallas kernels: 116 us -> 126 us
  local copies, waits for them, and re-layouts: 11.8 us -> 4.77 us
  blocking collectives: 2.45 us -> 0 us
    all_gather x2 -> x0, waiting for transfers between devices: 45.1 us -> none  [the longest x1 45.1 us: on_device(): shared = lax.all_gather(shared, 'mp', axis=1, tiled=True)]
    pallas_call x1, Pallas kernels: 47.2 us -> 57.6 us  [scatter_sum(): pl.pallas_call(functools.partial(scatter_kernel, n), in_specs=[pl.BlockSp...]
    transpose x1 -> x0, local copies, waits for them, and re-layouts: 4.06 us -> none  [on_device(): result = fold_and_project(ranks, member, rot_in.T, rot_out, eigen, rows_b...]
    slice x4 -> x1, local copies, waits for them, and re-layouts: 3.97 us -> 0.76 us  [on_device(): rows = basis_in[:OUT_ROWS]]
    all_gather x1 -> x0, blocking collectives: 2.45 us -> none  [on_device(): grads_all = lax.all_gather(out_grads, 'dp', axis=0, tiled=True)]
  transfers between devices with their start and end apart: 2 -> 0, of which waited for: 1 -> 0; matrix products, arithmetic and copies ran while one was open for 1% -> 0% of each run, Pallas kernels for 24% -> 0%
where the time goes in v4:
time: 137 us
  Pallas kernels  126 us (92%)
  local copies, waits for them, and re-layouts  4.77 us (3%)
  matrix products  3.48 us (3%)
  other arithmetic  2.25 us (2%)
    pallas_call x1, Pallas kernels, fold_and_project(): pl.pallas_call(functools.partial(fold_kernel, n), in_specs=[vmem, vmem, v...  68.9 us
    pallas_call x1, Pallas kernels, scatter_sum(): pl.pallas_call(functools.partial(scatter_kernel, n), in_specs=[pl.BlockSp...  57.6 us
    unnamed x9, local copies, waits for them, and re-layouts  4.01 us
    dot_general x1, matrix products, on_device(): lax.dot_general(basis_in, acts, (((0,), (1,)), ((), ())), preferred_eleme...  3.48 us

profile of v4, /device:TPU:0, one launch (start us, length us, event | category | flops | bytes accessed | tf_op | source)
XLA Modules:
  0.0 137.0 jit_solution(2300554288787501079)
XLA Ops:
  0.0 0.0 copy-start
  0.0 0.0 copy-start.1
  0.0 0.9 reduce-window.8
  0.9 0.7 bitcast_subtract_fusion
  1.6 0.8 slice.3.rows
  2.4 0.6 fusion.1.member
  3.0 0.0 copy-done
  3.0 3.5 %convolution_convert_fusion.feat_t = bf16[512,128]{1,0:T(8,128)(2,1)S(1)} fusion(bf16[4096,512]{1,0:T(8,128)(2,1)} %param.8, bf16[128,4096]{1,0:T(8,128)(2,1)S(1)} %copy-done), kind=kOutput, calls=%fused_computation | convolution fusion | flops 536936448 | bytes 5373952 | tf_op jit(solution)/shard_map/dot_general | solution.py:509
  6.5 0.0 copy-done.1
  6.5 57.6 %shard_map.64 = (bf16[256,896]{1,0:T(8,128)(2,1)S(1)}, bf16[8,576,256]{2,1,0:T(8,128)(2,1)S(1)}) custom-call(bf16[128,1792]{1,0:T(8,128)(2,1)S(1)} %copy-done.1, bf16[512,128]{1,0:T(8,128)(2,1)S(1)} %convolution_convert_fusion.feat_t, bf16[32,512]{1,0:T(8,128)(2,1)S(1)} %slice.3.rows, bf16[1792,7168]{1,0:T(8,128)(2,1)} %panel.3), custom_call_target="tpu_custom_call" | custom-call | flops 6576668672 | bytes 25690112 | tf_op jit(solution)/shard_map/pallas_call | solution.py:221
  64.1 0.0 copy-start.2
  64.1 1.4 %copy-done.2 = bf16[8,576,256]{2,1,0:T(8,128)(2,1)} copy-done((bf16[8,576,256]{2,1,0:T(8,128)(2,1)}, bf16[8,576,256]{2,1,0:T(8,128)(2,1)S(1)}, u32[]{:S(2)}) %copy-start.2) | copy-done | bytes 2359320
  65.5 0.0 copy-start.3
  65.5 0.8 copy-done.3
  66.3 68.9 %shard_map.65 = bf16[256,896]{1,0:T(8,128)(2,1)} custom-call(bf16[256,8]{1,0:T(8,128)(2,1)} %fusion.1.member, bf16[8,576,256]{2,1,0:T(8,128)(2,1)} %copy-done.2, bf16[256,896]{1,0:T(8,128)(2,1)} %copy-done.3, f32[4096,896]{1,0:T(8,128)} %eigen.1, bf16[1792,7168]{1,0:T(8,128)(2,1)} %panel.3), custom_call_target="tpu_custom_call" | custom-call | flops 30064771072 | bytes 40370176 | tf_op jit(solution)/shard_map/pallas_call | solution.py:461
  135.2 1.8 %copy.9 = bf16[8,32,896]{2,1,0:T(8,128)(2,1)} copy(bf16[8,32,896]{2,1,0:T(8,128)(2,1)} %bitcast.6) | data formatting | bytes 917504
Async XLA Ops:
  0.0 3.0 %copy-start = (bf16[128,4096]{1,0:T(8,128)(2,1)S(1)}, bf16[128,4096]{1,0:T(8,128)(2,1)}, u32[]{:S(2)}) copy-start(bf16[128,4096]{1,0:T(8,128)(2,1)} %param.6) | copy-start | bytes 3145732
  0.0 6.5 %copy-start.1 = (bf16[128,1792]{1,0:T(8,128)(2,1)S(1)}, bf16[128,1792]{1,0:T(8,128)(2,1)}, u32[]{:S(2)}) copy-start(bf16[128,1792]{1,0:T(8,128)(2,1)} %grads_own.1) | copy-start | bytes 1376260
  64.1 1.4 %copy-start.2 = (bf16[8,576,256]{2,1,0:T(8,128)(2,1)}, bf16[8,576,256]{2,1,0:T(8,128)(2,1)S(1)}, u32[]{:S(2)}) copy-start(bf16[8,576,256]{2,1,0:T(8,128)(2,1)S(1)} %get-tuple-element.7.shared) | copy-start | bytes 7077892
  65.5 0.8 copy-start.3

commit v5 on v4

--- a/solution.py
+++ b/solution.py
@@ -32,7 +32,7 @@
         return jnp.where(2 * z < half, rising, falling)
 
     def block_copy(i, j):
-        lane = jnp.where(j == 0, 1 - y, y)
+        lane = 1 - y if j == 0 else y
         start = pl.multiple_of((row(i) * 2 + lane) * cols, 128)
         return pltpu.make_async_copy(
             panel.at[:, pl.ds(start, cols)], blocks.at[2 * i + j], block_sem.at[2 * i + j]
@@ -98,9 +98,12 @@
                 item_copy(slot, 0).wait_recv()
                 onward(slot, False, True)
 
-    for i in range(half):
-        for j in range(2):
-            block_copy(i, j).start()
+    def taken(order):
+        block_copy(order // 2, order % 2).wait()
+        if order + 3 < n:
+            block_copy((order + 3) // 2, (order + 3) % 2).start()
+
+    block_copy(0, 0).start()
     shared[me, :feats, lanes] = feat_t[...]
     share = rows.shape[0] // 2
     for q in range(feats // 128):
@@ -117,15 +120,17 @@
     grads_copy.start()
     item_copy(me, 0).start()
     onward(me, True, True)
+    block_copy(0, 1).start()
+    block_copy(1, 0).start()
     grads_copy.wait_recv()
 
     def products(i):
-        block_copy(i, 0).wait()
+        taken(2 * i)
         ysend[i] = jnp.dot(
             grads[...], blocks[2 * i], preferred_element_type=F32
         ).astype(BF16)
         y_copy(i).start()
-        block_copy(i, 1).wait()
+        taken(2 * i + 1)
         own[i] = jnp.dot(grads[...], blocks[2 * i + 1], preferred_element_type=F32)
 
     for i in range(half):
@@ -266,12 +271,12 @@
 
 def fold_kernel(
     n, member, shared, rot_out, eigen, panel, out,
-    eig, blocks, masked, total, acc, swap, rows_back, *rest,
+    eig, masked, total, acc, swap, rows_back, *rest,
 ):
     parts = spans(out.shape[1])
     chunks = len(parts)
-    held = rest[:chunks]
-    eig_sem, block_sem, send_sem, recv_sem, swap_send, swap_recv = rest[chunks:]
+    held, blocks = rest[:chunks], rest[chunks : 2 * chunks]
+    eig_sem, block_sem, send_sem, recv_sem, swap_send, swap_recv = rest[2 * chunks :]
     feats, cols = eigen.shape
     seqs, rows = member.shape[1], rows_back.shape[0]
     half = n // 2
@@ -281,28 +286,42 @@
     partner, above, below = me + 1 - 2 * y, me + 2, me - 2
     has_above, has_below = z < half - 1, z > 0
 
-    def eig_copy(c):
+    def eig_copy(c, part):
         start, width = parts[c]
-        span = pl.ds(start, width)
-        return pltpu.make_async_copy(eigen.at[:, span], eig.at[:, span], eig_sem.at[c])
-
-    def block_copy(d):
-        start = pl.multiple_of(d * cols, 128)
+        at = (pl.ds(part * (feats // 2), feats // 2), pl.ds(start, width))
+        return pltpu.make_async_copy(eigen.at[at], eig.at[at], eig_sem.at[c, part])
+
+    def block_copy(c, d):
+        start, width = parts[c]
         return pltpu.make_async_copy(
-            panel.at[:, pl.ds(start, cols)], blocks.at[d], block_sem.at[d]
-        )
+            panel.at[:, pl.ds(d * cols + start, width)],
+            blocks[c].at[:, pl.ds(d * width, width)],
+            block_sem.at[c, d],
+        )
+
+    def load(unit):
+        if unit + 1 < chunks:
+            for part in range(2):
+                eig_copy(unit + 1, part).start()
+        elif unit + 1 < 2 * chunks:
+            for d in range(n):
+                block_copy(unit + 1 - chunks, d).start()
+
+    def held_slot(c, slot):
+        width = parts[c][1]
+        return held[c].at[:, pl.ds(pl.multiple_of(slot * width, 128), width)]
 
     def pass_on(c, place, kind):
         slot = place * 2 + y
         return pltpu.make_async_remote_copy(
-            src_ref=held[c].at[slot], dst_ref=held[c].at[slot],
+            src_ref=held_slot(c, slot), dst_ref=held_slot(c, slot),
             send_sem=send_sem.at[c, place, kind], recv_sem=recv_sem.at[c, slot],
             device_id={"mp": (partner, above, below)[kind]}, device_id_type=MESH,
         )
 
     def arrived(c, slot):
         pltpu.make_async_remote_copy(
-            src_ref=held[c].at[slot], dst_ref=held[c].at[slot],
+            src_ref=held_slot(c, slot), dst_ref=held_slot(c, slot),
             send_sem=send_sem.at[c, 0, 0], recv_sem=recv_sem.at[c, slot],
             device_id={"mp": partner}, device_id_type=MESH,
         ).wait_recv()
@@ -364,29 +383,24 @@
 
         lax.fori_loop(low, high, body, 0)
 
-    def project(c, low, high, part, wait):
-        start, width = parts[c]
-        at = pl.ds(pl.multiple_of(part * cols, 128), cols)
-
-        def body(d, carry):
-            if wait:
-
-                @pl.when(lax.rem(d, 2) != y)
+    def project(c, part, first):
+        if first:
+            for d in range(n):
+                block_copy(c, d).wait()
+
+                @pl.when(d % 2 != y)
                 def _():
                     arrived(c, d)
 
-            acc[part] += lax.dot_general(
-                held[c][d], blocks[d, at, start : start + width],
-                (((1,), (1,)), ((), ())), preferred_element_type=F32,
-            )
-            return carry
-
-        lax.fori_loop(low, high, body, 0)
-
-    for c in range(chunks):
-        eig_copy(c).start()
-    for d in range(n):
-        block_copy(d).start()
+        at = pl.ds(pl.multiple_of(part * cols, 128), cols)
+        product = lax.dot_general(
+            held[c][...], blocks[c][at, :], (((1,), (1,)), ((), ())),
+            preferred_element_type=F32,
+        )
+        acc[part] = product if c == 0 else acc[part] + product
+
+    for part in range(2):
+        eig_copy(0, part).start()
     for d in range(n):
         for half_row in range(2):
             for q in range(block // 128):
@@ -404,36 +418,36 @@
                 rot_out[:, start : start + width] * member[:, s : s + 1]
             )
         total[...] = jnp.zeros_like(total)
-        eig_copy(c).wait()
+        eig_copy(c, 0).wait()
+        load(2 * c)
         fold_part(c, 0, steps // 2)
         events(2 * c + 1)
+        eig_copy(c, 1).wait()
+        load(2 * c + 1)
         fold_part(c, steps // 2, steps)
         for s in range(seqs):
-            held[c][me, s * rows : (s + 1) * rows, :] = total[
+            mine = pl.ds(pl.multiple_of(me * width, 128), width)
+            held[c][s * rows : (s + 1) * rows, mine] = total[
                 :, s * width : (s + 1) * width
             ].astype(BF16)
         events(2 * c + 2)
 
-    for d in range(n):
-        block_copy(d).wait()
-    acc[...] = jnp.zeros_like(acc)
     unit = 2 * chunks
     for c in range(chunks - 1):
-        for low, high in ((0, half), (half, n)):
-            project(c, low, high, 0, True)
-            project(c, low, high, 1, False)
+        for part in range(2):
+            project(c, part, part == 0)
             unit += 1
             events(unit)
     last = chunks - 1
     for later in range(unit + 1, 2 * chunks + half):
         events(later)
-    project(last, 0, n, 1 - core, True)
+    project(last, 1 - core, True)
     exchange = pltpu.make_async_remote_copy(
         src_ref=acc.at[1 - core], dst_ref=swap, send_sem=swap_send, recv_sem=swap_recv,
         device_id={"dp": 1 - core}, device_id_type=MESH,
     )
     exchange.start()
-    project(last, 0, n, core, False)
+    project(last, core, False)
     exchange.wait()
     out[...] = (acc[core] + swap[...]).astype(BF16)
 
@@ -465,15 +479,15 @@
         out_shape=jax.ShapeDtypeStruct((seqs * rows, cols), BF16),
         scratch_shapes=[
             pltpu.VMEM((feats, cols), F32),
-            pltpu.VMEM((n, depth, cols), BF16),
             pltpu.VMEM((tokens, seqs * widest), BF16),
             pltpu.VMEM((rows, seqs * widest), F32),
             pltpu.VMEM((2, seqs * rows, cols), F32),
             pltpu.VMEM((seqs * rows, cols), F32),
             pltpu.VMEM((rows, feats), BF16),
-            *[pltpu.VMEM((n, seqs * rows, width), BF16) for _, width in parts],
-            pltpu.SemaphoreType.DMA((len(parts),)),
-            pltpu.SemaphoreType.DMA((n,)),
+            *[pltpu.VMEM((seqs * rows, n * width), BF16) for _, width in parts],
+            *[pltpu.VMEM((depth, n * width), BF16) for _, width in parts],
+            pltpu.SemaphoreType.DMA((len(parts), 2)),
+            pltpu.SemaphoreType.DMA((len(parts), n)),
             pltpu.SemaphoreType.DMA((len(parts), n // 2, 3)),
             pltpu.SemaphoreType.DMA((len(parts), n)),
             pltpu.SemaphoreType.DMA,

time: 137 us -> 130 us (0.949)
  Pallas kernels: 126 us -> 119 us
    pallas_call x1, Pallas kernels: 68.9 us -> 61.9 us  [fold_and_project(): pl.pallas_call(functools.partial(fold_kernel, n), in_specs=[vmem, vmem, v...]
where the time goes in v5:
time: 130 us
  Pallas kernels  119 us (92%)
  local copies, waits for them, and re-layouts  4.77 us (4%)
  matrix products  3.48 us (3%)
  other arithmetic  2.25 us (2%)
    pallas_call x1, Pallas kernels, fold_and_project(): pl.pallas_call(functools.partial(fold_kernel, n), in_specs=[vmem, vmem, v...  61.9 us
    pallas_call x1, Pallas kernels, scatter_sum(): pl.pallas_call(functools.partial(scatter_kernel, n), in_specs=[pl.BlockSp...  57.6 us
    unnamed x9, local copies, waits for them, and re-layouts  4.01 us
    dot_general x1, matrix products, on_device(): lax.dot_general(basis_in, acts, (((0,), (1,)), ((), ())), preferred_eleme...  3.48 us

profile of v5, /device:TPU:0, one launch (start us, length us, event | category | flops | bytes accessed | tf_op | source)
XLA Modules:
  0.0 130.0 jit_solution(9622831413867539719)
XLA Ops:
  0.0 0.0 copy-start
  0.0 0.0 copy-start.1
  0.0 0.9 reduce-window.8
  0.9 0.7 bitcast_subtract_fusion
  1.6 0.8 slice.3.rows
  2.4 0.6 fusion.1.member
  3.0 0.0 copy-done
  3.0 3.5 %convolution_convert_fusion.feat_t = bf16[512,128]{1,0:T(8,128)(2,1)S(1)} fusion(bf16[4096,512]{1,0:T(8,128)(2,1)} %param.8, bf16[128,4096]{1,0:T(8,128)(2,1)S(1)} %copy-done), kind=kOutput, calls=%fused_computation | convolution fusion | flops 536936448 | bytes 5373952 | tf_op jit(solution)/shard_map/dot_general | solution.py:523
  6.5 0.0 copy-done.1
  6.5 57.6 %shard_map.64 = (bf16[256,896]{1,0:T(8,128)(2,1)S(1)}, bf16[8,576,256]{2,1,0:T(8,128)(2,1)S(1)}) custom-call(bf16[128,1792]{1,0:T(8,128)(2,1)S(1)} %copy-done.1, bf16[512,128]{1,0:T(8,128)(2,1)S(1)} %convolution_convert_fusion.feat_t, bf16[32,512]{1,0:T(8,128)(2,1)S(1)} %slice.3.rows, bf16[1792,7168]{1,0:T(8,128)(2,1)} %panel.3), custom_call_target="tpu_custom_call" | custom-call | flops 6576668672 | bytes 25690112 | tf_op jit(solution)/shard_map/pallas_call | solution.py:226
  64.1 0.0 copy-start.2
  64.1 1.4 %copy-done.2 = bf16[8,576,256]{2,1,0:T(8,128)(2,1)} copy-done((bf16[8,576,256]{2,1,0:T(8,128)(2,1)}, bf16[8,576,256]{2,1,0:T(8,128)(2,1)S(1)}, u32[]{:S(2)}) %copy-start.2) | copy-done | bytes 2359320
  65.5 0.0 copy-start.3
  65.5 0.8 copy-done.3
  66.3 61.9 %shard_map.65 = bf16[256,896]{1,0:T(8,128)(2,1)} custom-call(bf16[256,8]{1,0:T(8,128)(2,1)} %fusion.1.member, bf16[8,576,256]{2,1,0:T(8,128)(2,1)} %copy-done.2, bf16[256,896]{1,0:T(8,128)(2,1)} %copy-done.3, f32[4096,896]{1,0:T(8,128)} %eigen.1, bf16[1792,7168]{1,0:T(8,128)(2,1)} %panel.3), custom_call_target="tpu_custom_call" | custom-call | flops 30064771072 | bytes 40370176 | tf_op jit(solution)/shard_map/pallas_call | solution.py:475
  128.2 1.8 %copy.9 = bf16[8,32,896]{2,1,0:T(8,128)(2,1)} copy(bf16[8,32,896]{2,1,0:T(8,128)(2,1)} %bitcast.6) | data formatting | bytes 917504
Async XLA Ops:
  0.0 3.0 %copy-start = (bf16[128,4096]{1,0:T(8,128)(2,1)S(1)}, bf16[128,4096]{1,0:T(8,128)(2,1)}, u32[]{:S(2)}) copy-start(bf16[128,4096]{1,0:T(8,128)(2,1)} %param.6) | copy-start | bytes 3145732
  0.0 6.5 %copy-start.1 = (bf16[128,1792]{1,0:T(8,128)(2,1)S(1)}, bf16[128,1792]{1,0:T(8,128)(2,1)}, u32[]{:S(2)}) copy-start(bf16[128,1792]{1,0:T(8,128)(2,1)} %grads_own.1) | copy-start | bytes 1376260
  64.1 1.4 %copy-start.2 = (bf16[8,576,256]{2,1,0:T(8,128)(2,1)}, bf16[8,576,256]{2,1,0:T(8,128)(2,1)S(1)}, u32[]{:S(2)}) copy-start(bf16[8,576,256]{2,1,0:T(8,128)(2,1)S(1)} %get-tuple-element.7.shared) | copy-start | bytes 7077892
  65.5 0.8 copy-start.3

commit v6 on v5

--- a/solution.py
+++ b/solution.py
@@ -265,8 +265,13 @@
     )(grads, feat_t, rows, panel)
 
 
-def spans(cols, width=256):
-    return [(start, min(width, cols - start)) for start in range(0, cols, width)]
+def spans(cols):
+    parts, start = [(0, 128)], 128
+    while start < cols:
+        width = 256 if cols - start > 256 else 128
+        parts.append((start, width))
+        start += width
+    return parts
 
 
 def fold_kernel(

time: 130 us -> 132 us (1.015)
  Pallas kernels: 119 us -> 121 us
    pallas_call x1, Pallas kernels: 61.9 us -> 63.4 us  [fold_and_project(): pl.pallas_call(functools.partial(fold_kernel, n), in_specs=[vmem, vmem, v...]
where the time goes in v6:
time: 132 us; the launch traced here: 131 us
  Pallas kernels  121 us (92%)
  local copies, waits for them, and re-layouts  4.77 us (4%)
  matrix products  3.48 us (3%)
  other arithmetic  2.25 us (2%)
    pallas_call x1, Pallas kernels, fold_and_project(): pl.pallas_call(functools.partial(fold_kernel, n), in_specs=[vmem, vmem, v...  63.4 us
    pallas_call x1, Pallas kernels, scatter_sum(): pl.pallas_call(functools.partial(scatter_kernel, n), in_specs=[pl.BlockSp...  57.6 us
    unnamed x9, local copies, waits for them, and re-layouts  4.01 us
    dot_general x1, matrix products, on_device(): lax.dot_general(basis_in, acts, (((0,), (1,)), ((), ())), preferred_eleme...  3.48 us

profile of v6, /device:TPU:0, one launch (start us, length us, event | category | flops | bytes accessed | tf_op | source)
XLA Modules:
  0.0 131.5 jit_solution(18013189287252431801)
XLA Ops:
  0.0 0.0 copy-start
  0.0 0.0 copy-start.1
  0.0 0.9 reduce-window.8
  0.9 0.7 bitcast_subtract_fusion
  1.6 0.8 slice.3.rows
  2.4 0.6 fusion.1.member
  3.0 0.0 copy-done
  3.0 3.5 %convolution_convert_fusion.feat_t = bf16[512,128]{1,0:T(8,128)(2,1)S(1)} fusion(bf16[4096,512]{1,0:T(8,128)(2,1)} %param.8, bf16[128,4096]{1,0:T(8,128)(2,1)S(1)} %copy-done), kind=kOutput, calls=%fused_computation | convolution fusion | flops 536936448 | bytes 5373952 | tf_op jit(solution)/shard_map/dot_general | solution.py:528
  6.5 0.0 copy-done.1
  6.5 57.6 %shard_map.64 = (bf16[256,896]{1,0:T(8,128)(2,1)S(1)}, bf16[8,576,256]{2,1,0:T(8,128)(2,1)S(1)}) custom-call(bf16[128,1792]{1,0:T(8,128)(2,1)S(1)} %copy-done.1, bf16[512,128]{1,0:T(8,128)(2,1)S(1)} %convolution_convert_fusion.feat_t, bf16[32,512]{1,0:T(8,128)(2,1)S(1)} %slice.3.rows, bf16[1792,7168]{1,0:T(8,128)(2,1)} %panel.3), custom_call_target="tpu_custom_call" | custom-call | flops 6576668672 | bytes 25690112 | tf_op jit(solution)/shard_map/pallas_call | solution.py:226
  64.1 0.0 copy-start.2
  64.1 1.4 %copy-done.2 = bf16[8,576,256]{2,1,0:T(8,128)(2,1)} copy-done((bf16[8,576,256]{2,1,0:T(8,128)(2,1)}, bf16[8,576,256]{2,1,0:T(8,128)(2,1)S(1)}, u32[]{:S(2)}) %copy-start.2) | copy-done | bytes 2359320
  65.5 0.0 copy-start.3
  65.5 0.8 copy-done.3
  66.3 63.4 %shard_map.65 = bf16[256,896]{1,0:T(8,128)(2,1)} custom-call(bf16[256,8]{1,0:T(8,128)(2,1)} %fusion.1.member, bf16[8,576,256]{2,1,0:T(8,128)(2,1)} %copy-done.2, bf16[256,896]{1,0:T(8,128)(2,1)} %copy-done.3, f32[4096,896]{1,0:T(8,128)} %eigen.1, bf16[1792,7168]{1,0:T(8,128)(2,1)} %panel.3), custom_call_target="tpu_custom_call" | custom-call | flops 30064771072 | bytes 40370176 | tf_op jit(solution)/shard_map/pallas_call | solution.py:480
  129.7 1.8 %copy.9 = bf16[8,32,896]{2,1,0:T(8,128)(2,1)} copy(bf16[8,32,896]{2,1,0:T(8,128)(2,1)} %bitcast.6) | data formatting | bytes 917504
Async XLA Ops:
  0.0 3.0 %copy-start = (bf16[128,4096]{1,0:T(8,128)(2,1)S(1)}, bf16[128,4096]{1,0:T(8,128)(2,1)}, u32[]{:S(2)}) copy-start(bf16[128,4096]{1,0:T(8,128)(2,1)} %param.6) | copy-start | bytes 3145732
  0.0 6.5 %copy-start.1 = (bf16[128,1792]{1,0:T(8,128)(2,1)S(1)}, bf16[128,1792]{1,0:T(8,128)(2,1)}, u32[]{:S(2)}) copy-start(bf16[128,1792]{1,0:T(8,128)(2,1)} %grads_own.1) | copy-start | bytes 1376260
  64.1 1.4 %copy-start.2 = (bf16[8,576,256]{2,1,0:T(8,128)(2,1)}, bf16[8,576,256]{2,1,0:T(8,128)(2,1)S(1)}, u32[]{:S(2)}) copy-start(bf16[8,576,256]{2,1,0:T(8,128)(2,1)S(1)} %get-tuple-element.7.shared) | copy-start | bytes 7077892
  65.5 0.8 copy-start.3
